TPU v7x, 32 devices: a whole 2x2x4 slice. The times are simulated.
32 devices in a mesh: section: 2 (over x), dec: 4 (over z), row: 4 (over y, core).
Axes of the slice: x: 2, y: 2, z: 4, core: 2. Of those that a mesh axis runs over, the one named last changes fastest.
Arguments:
- hidden: bfloat16 [8, 4, 16, 8, 5120], P('dec', None, 'row', None, 'section'), may hold values from -12 to 12
- head_weight: bfloat16 [5120, 64], P('section'), may hold values from -0.078125 to 0.078125
- head_bias: float32 [64], replicated, may hold values from -3 to 3
- lat_cache: bfloat16 [8, 2, 32, 16, 16], P('dec', None, 'row'), may hold values from -6 to 6
- mid_cache: bfloat16 [8, 2, 32, 16, 512], P('dec', None, 'row', None, 'section'), may hold values from -6 to 6
- moves: int32 [8], replicated, may hold values from 0 to 7, each once
- span_index: int32 [8], P('dec'), may hold values from 0 to 3
- conv_in_weight: bfloat16 [3, 3, 3, 16, 512], P(None, None, None, None, 'section'), may hold values from -0.3125 to 0.3125
- conv_in_bias: float32 [512], P('section'), may hold values from -3 to 3
- gn_gain: float32 [512], P('section'), may hold values from 0.25 to 1.75
- gn_bias: float32 [512], P('section'), may hold values from -3 to 3
- mid_weight: bfloat16 [3, 3, 3, 512, 512], P(None, None, None, None, 'section'), may hold values from -0.0546875 to 0.0546875
- mid_bias: float32 [512], P('section'), may hold values from -3 to 3
Outputs:
- decoded: bfloat16 [8, 4, 32, 16, 512], P('dec', None, 'row', None, 'section')
- new_lat_cache: bfloat16 [8, 2, 32, 16, 16], P('dec', None, 'row')
- new_mid_cache: bfloat16 [8, 2, 32, 16, 512], P('dec', None, 'row', None, 'section')
Inputs may be any that keep to these rules, and one draw needn't show every extreme that they name: moves holds each of the 8 slots once.
All inputs are finite; a program needn't handle non-finite values.
Results may differ from a plain program's by a relative error of at most 0.012.
Values may be sent and summed in bfloat16 or wider, within the bound.
A program may use at most 128 MiB of HBM per device.

v0:
```python
import jax
import jax.numpy as jnp
from jax import lax
from jax.sharding import PartitionSpec as P

CZ = 16
C = 512
GROUPS = 32
CACHE = 2


def extended(block, sides, width):
    for axis, dim in sides:
        count = lax.axis_size(axis)
        forward = [(i, i + 1) for i in range(count - 1)]
        backward = [(target, source) for source, target in forward]
        low = lax.ppermute(
            lax.slice_in_dim(block, block.shape[dim] - width, None, axis=dim), axis, forward
        )
        high = lax.ppermute(lax.slice_in_dim(block, 0, width, axis=dim), axis, backward)
        block = jnp.concatenate([low, block, high], axis=dim)
    return block


def tap_sum(padded, weight, frames, rows, cols, total):
    cin = padded.shape[-1]
    for a in range(3):
        for b in range(3):
            for e in range(3):
                tap = padded[:, a : a + frames, b : b + rows, e : e + cols].reshape(-1, cin)
                total = total + jnp.dot(tap, weight[a, b, e], preferred_element_type=jnp.float32)
    return total


def shards(
    hidden,
    head_weight,
    head_bias,
    lat_cache,
    mid_cache,
    moves,
    span_index,
    conv_in_weight,
    conv_in_bias,
    gn_gain,
    gn_bias,
    mid_weight,
    mid_bias,
):
    local_streams, frames, half_rows, half_cols, width_part = hidden.shape
    rows = 2 * half_rows
    cols = 2 * half_cols
    partial_patch = jnp.dot(
        hidden.reshape(-1, width_part), head_weight, preferred_element_type=jnp.float32
    )
    patches = lax.psum(partial_patch, "section") + head_bias
    latent = patches.reshape(local_streams, frames, half_rows, half_cols, 2, 2, CZ)
    latent = (
        latent.transpose(0, 1, 2, 4, 3, 5, 6)
        .reshape(local_streams, frames, rows, cols, CZ)
        .astype(jnp.bfloat16)
    )
    slots = lax.axis_index("dec") * local_streams + lax.iota(jnp.int32, local_streams)
    sources = jnp.take(moves, slots, axis=0)
    pieces = (
        lax.all_gather(lat_cache, "dec", axis=0, tiled=True),
        lax.all_gather(mid_cache, "dec", axis=0, tiled=True),
    )
    count = pieces[0].shape[0]
    select = (sources[:, None] == lax.iota(jnp.int32, count)[None, :]).astype(jnp.bfloat16)
    lat_pick = jnp.einsum(
        "kr,rtabc->ktabc", select, pieces[0], preferred_element_type=jnp.float32
    ).astype(jnp.bfloat16)
    mid_pick = jnp.einsum(
        "kr,rtabc->ktabc", select, pieces[1], preferred_element_type=jnp.float32
    ).astype(jnp.bfloat16)
    prev_lat = lat_pick
    prev_mid = mid_pick
    live = (span_index > 0).astype(jnp.bfloat16)[:, None, None, None, None]
    prev_lat = prev_lat * live
    prev_mid = prev_mid * live
    x_in = jnp.concatenate([prev_lat, latent], 1)
    depth = x_in.shape[1]
    x_flat = x_in.reshape(local_streams, depth, rows, cols * CZ)
    x_rim = extended(x_flat, (("row", 2),), 1)
    x_pad = jnp.pad(
        x_rim.reshape(local_streams, depth, rows + 2, cols, CZ),
        ((0, 0), (0, 0), (0, 0), (1, 1), (0, 0)),
    )
    channel_part = conv_in_weight.shape[-1]
    first_total = jnp.zeros((local_streams * frames * rows * cols, channel_part), jnp.float32)
    first = (tap_sum(x_pad, conv_in_weight, frames, rows, cols, first_total) + conv_in_bias).astype(
        jnp.bfloat16
    )
    group_size = C // GROUPS
    local_groups = channel_part // group_size
    grouped = first.astype(jnp.float32).reshape(
        local_streams, frames * rows * cols, local_groups, group_size
    )
    group_sum, group_sq = lax.psum(
        (jnp.sum(grouped, (1, 3)), jnp.sum(grouped * grouped, (1, 3))), "row"
    )
    count = frames * rows * lax.axis_size("row") * cols * group_size
    gmean = (group_sum / count)[:, None, :, None]
    gvar = (group_sq / count)[:, None, :, None] - gmean * gmean
    scaled = ((grouped - gmean) * lax.rsqrt(gvar + 1e-05)).reshape(
        local_streams, -1, channel_part
    ) * gn_gain + gn_bias
    act = (
        jax.nn.silu(scaled)
        .astype(jnp.bfloat16)
        .reshape(local_streams, frames, rows, cols, channel_part)
    )
    m_in = jnp.concatenate([prev_mid, act], 1)
    m_rim = extended(m_in, (("row", 2),), 1)
    m_pad = jnp.pad(m_rim, ((0, 0), (0, 0), (0, 0), (1, 1), (0, 0)))
    conv_start = jnp.zeros((local_streams * frames * rows * cols, channel_part), jnp.float32)
    conv = tap_sum(
        lax.all_gather(m_pad, "section", axis=4, tiled=True),
        mid_weight,
        frames,
        rows,
        cols,
        conv_start,
    )
    decoded = (first.astype(jnp.float32) + conv + mid_bias).astype(jnp.bfloat16)
    decoded = decoded.reshape(local_streams, frames, rows, cols, channel_part)
    return (decoded, latent[:, frames - CACHE :], act[:, frames - CACHE :])


def solution(mesh):
    placed = (
        P("dec", None, "row", None, "section"),
        P("section", None),
        P(),
        P("dec", None, "row", None, None),
        P("dec", None, "row", None, "section"),
        P(),
        P("dec"),
        P(None, None, None, None, "section"),
        P("section"),
        P("section"),
        P("section"),
        P(None, None, None, None, "section"),
        P("section"),
    )
    return jax.shard_map(
        shards,
        mesh=mesh,
        in_specs=placed,
        out_specs=(
            P("dec", None, "row", None, "section"),
            P("dec", None, "row", None, None),
            P("dec", None, "row", None, "section"),
        ),
        check_vma=False,
    )
```

profile of v0, /device:TPU:0, one launch (start us, length us, event | category | flops | bytes accessed | tf_op | source)
XLA Modules:
  0.0 169.3 jit_solution(11122233249182555263)
XLA Ops:
  8.1 1.3 copy-done
  9.3 2.1 %fusion.142 = f32[256,64]{0,1:T(8,128)} fusion(bf16[256,2560]{1,0:T(8,128)(2,1)S(1)} %bitcast.294, bf16[2560,64]{0,1:T(8,128)(2,1)} %param.14), kind=kOutput, calls=%fused_computation.225 | convolution fusion | flops 83886080 | bytes 1703936 | tf_op jit(solution)/shard_map/dot_general | solution.py:53
  11.5 0.5 all-gather.3.cloned.1.call-update
  12.1 0.7 compare_convert_fusion
  12.8 1.3 gather_fusion
  14.1 22.1 %all_gather.9 = bf16[8,2,8,16,16]{4,3,2,1,0:T(8,128)(2,1)S(1)} all-gather(bf16[2,2,8,16,16]{4,3,2,1,0:T(8,128)(2,1)} %param.16), channel_id=1, replica_groups=mesh['section'=2,'dec'=4,'row'=4] {'dec'}, dimensions={0}, use_global_device_ids=true | all-gather | bytes 81920 | tf_op jit(solution)/shard_map/all_gather | solution.py:66
  36.2 0.4 fusion.12
  36.7 0.9 add_convert_fusion
  38.6 1.3 collective-permute-start.1
  39.9 3.0 %collective-permute-start = (bf16[2,6,1,256]{3,0,1,2:T(2,128)(2,1)S(1)}, bf16[2,6,1,256]{3,0,1,2:T(2,128)(2,1)S(1)}, u32[]{:S(2)}, u32[]{:S(2)}) collective-permute-start(bf16[2,6,1,256]{3,0,1,2:T(2,128)(2,1)S(1)} %copy.83), channel_id=1, source_target_pairs={{0,1},{1,2},{2,3},{4,5},{5,6},{6,7},{8,9},{9,10},{10,11},{12,13},{... | collective-permute-start | bytes 18440 | tf_op jit(solution)/shard_map/ppermute | solution.py:17
  43.0 0.7 collective-permute-done
  44.5 1.1 fusion.138
  53.6 0.9 reshape.268
  54.5 0.8 fusion.135
  55.4 7.2 %all-reduce.2 = (f32[2,16]{1,0:T(2,128)S(1)}, f32[2,16]{1,0:T(2,128)S(1)}) all-reduce(f32[2,16]{1,0:T(2,128)S(1)} %copy.80, f32[2,16]{1,0:T(2,128)S(1)} %copy.79), channel_id=1, replica_groups=mesh['section'=2,'dec'=4,'row'=4] {'row'}, use_global_device_ids=true, to_apply=%region_4.5 | all-reduce | flops 64 | bytes 512 | tf_op jit(solution)/shard_map/psum | solution.py:100
  63.3 2.0 %fusion.11 = bf16[2,2,8,16,256]{4,0,3,2,1:T(2,128)(2,1)S(1)} fusion(bf16[8,2,8,16,256]{4,3,2,1,0:T(8,128)(2,1)} %all-gather.3.cloned.1.call-done, bf16[2]{0:T(256)(128)(2,1)S(1)} %compare_convert_fusion, s32[2]{0:T(128)S(1)} %and_select_fusion), kind=kOutput, calls=%fused_computation.71 | convolution fusion | flops 2359312 | bytes 1310732 | tf_op jit(solution)/shard_map/kr,rtabc->ktabc/dot_general | solution.py:74
  65.4 2.0 %collective-permute-start.2 = (bf16[2,6,1,16,256]{4,3,2,1,0:T(8,128)(2,1)S(1)}, bf16[2,6,1,16,256]{4,3,2,1,0:T(8,128)(2,1)S(1)}, u32[]{:S(2)}, u32[]{:S(2)}) collective-permute-start(bf16[2,6,1,16,256]{4,3,2,1,0:T(8,128)(2,1)S(1)} %get-tuple-element.34), channel_id=1, source_target_pairs={{0,1},{1,2},{2,3},{4,5},{5,6},{6,7},{8,9},{9,10},{10,11},{12,13},{... | collective-permute-start | bytes 294920 | tf_op jit(solution)/shard_map/ppermute | solution.py:17
  67.4 1.5 collective-permute-start.3
  68.8 3.2 %collective-permute-done.3 = bf16[2,6,1,16,256]{4,3,2,1,0:T(8,128)(2,1)S(1)} collective-permute-done((bf16[2,6,1,16,256]{4,3,2,1,0:T(8,128)(2,1)S(1)}, bf16[2,6,1,16,256]{4,3,2,1,0:T(8,128)(2,1)S(1)}, u32[]{:S(2)}, u32[]{:S(2)}) %collective-permute-start.3) | collective-permute-done | bytes 98336 | tf_op jit(solution)/shard_map/ppermute | solution.py:20
  72.0 2.0 %select_maximum_fusion = bf16[2,6,10,18,256]{4,3,2,1,0:T(8,128)(2,1)} fusion(bf16[2,6,1,16,256]{4,3,2,1,0:T(8,128)(2,1)S(1)} %collective-permute-done.3, bf16[2,6,1,16,256]{4,3,2,1,0:T(8,128)(2,1)S(1)} %collective-permute-done.2, bf16[2,4,8,16,256]{4,3,2,1,0:T(8,128)(2,1)S(1)} %multiply_convert_fusion, bf16[2,2,8,16,256]{4,3,2,1,0:T(8,128)(2,1)S(1)} %copy.81), kind=kLoop, calls=%fused_computation.6 | loop fusion | flops 8294400 | bytes 2088960 | tf_op jit(solution)/shard_map/concatenate | solution.py:21
  74.1 0.7 slice.530
  74.8 0.7 slice.531
  75.5 43.2 %all-gather.5.cloned.1.call-done = bf16[2,6,10,18,512]{4,3,2,1,0:T(8,128)(2,1)} async-done(((bf16[2,6,10,18,256]{4,3,2,1,0:T(8,128)(2,1)}), bf16[2,6,10,18,512]{4,3,2,1,0:T(8,128)(2,1)}) %all-gather.5.cloned.1.call-update) | async-done | bytes 2211856 | tf_op jit(solution)/shard_map/all_gather | solution.py:119
  118.7 6.5 %fusion.137 = (bf16[2,4,8,16,512]{4,3,2,1,0:T(8,128)(2,1)S(1)}, bf16[2,4,8,16,512]{4,3,2,1,0:T(8,128)(2,1)S(1)}, bf16[2,4,8,16,512]{4,3,2,1,0:T(8,128)(2,1)S(1)}...) fusion(bf16[2,6,10,18,512]{4,3,2,1,0:T(8,128)(2,1)} %all-gather, ...), kind=kLoop, calls=%fused_computation.220 | loop fusion | bytes 16777216 | tf_op jit(solution)/shard_map/slice | solution.py:30
  125.2 1.4 fusion.45
  126.5 1.4 convolution_add_fusion.25
  127.9 1.4 convolution_add_fusion.24
  129.3 1.4 convolution_add_fusion.23
  130.8 1.5 convolution_add_fusion.22
  132.3 1.4 convolution_add_fusion.21
  133.7 1.4 convolution_add_fusion.20
  135.1 2.4 %convolution_add_fusion.19 = f32[1024,256]{1,0:T(8,128)} fusion(f32[1024,256]{1,0:T(8,128)S(1)} %convolution_add_fusion.20, bf16[1024,512]{1,0:T(8,128)(2,1)S(1)} %bitcast.322, bf16[3,3,3,512,256]{4,3,2,1,0:T(8,128)(2,1)} %param.24), kind=kOutput, calls=%fused_computation.33 | convolution fusion | flops 268697600 | bytes 3407872 | tf_op jit(solution)/shard_map/dot_general | solution.py:31
  137.4 8.1 %fusion.136 = (bf16[2,4,8,16,512]{4,3,2,1,0:T(8,128)(2,1)S(1)}, bf16[2,4,8,16,512]{4,3,2,1,0:T(8,128)(2,1)S(1)}, bf16[2,4,8,16,512]{4,3,2,1,0:T(8,128)(2,1)}, bf...) fusion(bf16[2,6,10,18,512]{4,3,2,1,0:T(8,128)(2,1)S(1)} %copy-d, ...), kind=kLoop, calls=%fused_computation.219 | loop fusion | bytes 39845888 | tf_op jit(solution)/shard_map/slice | solution.py:30
  145.6 2.2 %convolution_add_fusion.18 = f32[1024,256]{1,0:T(8,128)S(1)} fusion(f32[1024,256]{1,0:T(8,128)} %convolution_add_fusion.19, bf16[1024,512]{1,0:T(8,128)(2,1)} %bitcast.323, bf16[3,3,3,512,256]{4,3,2,1,0:T(8,128)(2,1)} %param.24), kind=kOutput, calls=%fused_computation.32 | convolution fusion | flops 268697600 | bytes 3407872 | tf_op jit(solution)/shard_map/dot_general | solution.py:31
  147.8 2.3 %convolution_add_fusion.17 = f32[1024,256]{1,0:T(8,128)S(1)} fusion(f32[1024,256]{1,0:T(8,128)S(1)} %convolution_add_fusion.18, bf16[1024,512]{1,0:T(8,128)(2,1)} %bitcast.321, bf16[3,3,3,512,256]{4,3,2,1,0:T(8,128)(2,1)} %param.24), kind=kOutput, calls=%fused_computation.31 | convolution fusion | flops 268697600 | bytes 3407872 | tf_op jit(solution)/shard_map/dot_general | solution.py:31
  150.1 1.5 convolution_add_fusion.16
  151.7 1.5 convolution_add_fusion.15
  153.2 1.5 convolution_add_fusion.14
  154.7 0.4 convolution_add_fusion.13
  155.2 0.4 convolution_add_fusion.12
  155.6 0.4 convolution_add_fusion.11
  157.9 0.4 convolution_add_fusion.6
  158.4 0.4 convolution_add_fusion.5
  158.8 0.4 convolution_add_fusion.4
  159.3 0.4 convolution_add_fusion.3
  159.7 0.4 convolution_add_fusion.2
  160.2 0.4 convolution_add_fusion.1
  160.6 1.2 fusion.9
  (117 shorter events, 12.4 us)
Async XLA Ops:
  8.0 1.3 copy-start
  8.0 28.7 %all-reduce.5.cloned.1.call-start = ((), (), s32[]{:S(2)}) async-start(), calls=%async_computation | async-start | bytes 131072 | tf_op jit(solution)/shard_map/psum | solution.py:56
  11.5 51.9 %all-gather.3.cloned.1.call-start = ((), (), s32[]{:S(2)}) async-start(), calls=%async_computation.1 | async-start | bytes 1310720 | tf_op jit(solution)/shard_map/all_gather | solution.py:67
  12.0 106.6 %all-gather.5.cloned.1.call-start = ((), (), s32[]{:S(2)}) async-start(), calls=%async_computation.2 | async-start | bytes 4423680 | tf_op jit(solution)/shard_map/all_gather | solution.py:119
  38.6 5.3 %collective-permute-start.1 = (bf16[2,6,1,256]{3,0,1,2:T(2,128)(2,1)S(1)}, bf16[2,6,1,256]{3,0,1,2:T(2,128)(2,1)S(1)}, u32[]{:S(2)}, u32[]{:S(2)}) collective-permute-start(bf16[2,6,1,256]{3,0,1,2:T(2,128)(2,1)S(1)} %copy.84), channel_id=1, source_target_pairs={{1,0},{2,1},{3,2},{5,4},{6,5},{7,6},{9,8},{10,9},{11,10},{13,12},{... | collective-permute-start | bytes 18440 | tf_op jit(solution)/shard_map/ppermute | solution.py:20
  39.9 3.8 %collective-permute-start = (bf16[2,6,1,256]{3,0,1,2:T(2,128)(2,1)S(1)}, bf16[2,6,1,256]{3,0,1,2:T(2,128)(2,1)S(1)}, u32[]{:S(2)}, u32[]{:S(2)}) collective-permute-start(bf16[2,6,1,256]{3,0,1,2:T(2,128)(2,1)S(1)} %copy.83), channel_id=1, source_target_pairs={{0,1},{1,2},{2,3},{4,5},{5,6},{6,7},{8,9},{9,10},{10,11},{12,13},{... | collective-permute-start | bytes 18440 | tf_op jit(solution)/shard_map/ppermute | solution.py:17
  44.3 1.6 copy-start.17
  51.3 1.7 copy-start.18
  52.1 10.8 %copy-start.19 = (f32[256]{0:T(256)S(1)}, f32[256]{0:T(256)}, u32[]{:S(2)}) copy-start(f32[256]{0:T(256)} %param.23) | copy-start | bytes 3076
  52.1 10.8 %copy-start.20 = (f32[256]{0:T(256)S(1)}, f32[256]{0:T(256)}, u32[]{:S(2)}) copy-start(f32[256]{0:T(256)} %param.22) | copy-start | bytes 3076
  65.4 3.4 %collective-permute-start.2 = (bf16[2,6,1,16,256]{4,3,2,1,0:T(8,128)(2,1)S(1)}, bf16[2,6,1,16,256]{4,3,2,1,0:T(8,128)(2,1)S(1)}, u32[]{:S(2)}, u32[]{:S(2)}) collective-permute-start(bf16[2,6,1,16,256]{4,3,2,1,0:T(8,128)(2,1)S(1)} %get-tuple-element.34), channel_id=1, source_target_pairs={{0,1},{1,2},{2,3},{4,5},{5,6},{6,7},{8,9},{9,10},{10,11},{12,13},{... | collective-permute-start | bytes 294920 | tf_op jit(solution)/shard_map/ppermute | solution.py:17
  67.4 4.7 %collective-permute-start.3 = (bf16[2,6,1,16,256]{4,3,2,1,0:T(8,128)(2,1)S(1)}, bf16[2,6,1,16,256]{4,3,2,1,0:T(8,128)(2,1)S(1)}, u32[]{:S(2)}, u32[]{:S(2)}) collective-permute-start(bf16[2,6,1,16,256]{4,3,2,1,0:T(8,128)(2,1)S(1)} %get-tuple-element.35), channel_id=1, source_target_pairs={{1,0},{2,1},{3,2},{5,4},{6,5},{7,6},{9,8},{10,9},{11,10},{13,12},{... | collective-permute-start | bytes 294920 | tf_op jit(solution)/shard_map/ppermute | solution.py:20
  130.7 6.7 %copy-start.2 = (bf16[2,6,10,18,512]{4,3,2,1,0:T(8,128)(2,1)S(1)}, bf16[2,6,10,18,512]{4,3,2,1,0:T(8,128)(2,1)}, u32[]{:S(2)}) copy-start(bf16[2,6,10,18,512]{4,3,2,1,0:T(8,128)(2,1)} %all-gather.5.cloned.1.call-done) | copy-start | bytes 6635524
  145.5 4.6 %copy-start.16 = (bf16[2,4,8,16,512]{4,3,2,1,0:T(8,128)(2,1)S(1)}, bf16[2,4,8,16,512]{4,3,2,1,0:T(8,128)(2,1)}, u32[]{:S(2)}) copy-start(bf16[2,4,8,16,512]{4,3,2,1,0:T(8,128)(2,1)} %get-tuple-element.23) | copy-start | bytes 3145732
  145.5 6.1 %copy-start.15 = (bf16[2,4,8,16,512]{4,3,2,1,0:T(8,128)(2,1)S(1)}, bf16[2,4,8,16,512]{4,3,2,1,0:T(8,128)(2,1)}, u32[]{:S(2)}) copy-start(bf16[2,4,8,16,512]{4,3,2,1,0:T(8,128)(2,1)} %get-tuple-element.22) | copy-start | bytes 3145732
  145.6 7.6 %copy-start.14 = (bf16[2,4,8,16,512]{4,3,2,1,0:T(8,128)(2,1)S(1)}, bf16[2,4,8,16,512]{4,3,2,1,0:T(8,128)(2,1)}, u32[]{:S(2)}) copy-start(bf16[2,4,8,16,512]{4,3,2,1,0:T(8,128)(2,1)} %get-tuple-element.21) | copy-start | bytes 3145732
  145.6 9.1 %slice-start = ((s8[7077888]{0:T(1024)(128)(4,1)}), s8[4194304]{0:T(1024)(128)(4,1)S(1)}, s32[]{:S(2)}) async-start(s8[7077888]{0:T(1024)(128)(4,1)} %bitcast.302), calls=%async_computation.3 | async-start | bytes 8388608
  147.8 6.9 %copy-start.13 = (bf16[2,4,8,16,512]{4,3,2,1,0:T(8,128)(2,1)S(1)}, bf16[2,4,8,16,512]{4,3,2,1,0:T(8,128)(2,1)}, u32[]{:S(2)}) copy-start(bf16[2,4,8,16,512]{4,3,2,1,0:T(8,128)(2,1)} %get-tuple-element.20) | copy-start | bytes 3145732
  150.1 5.1 %copy-start.12 = (bf16[2,4,8,16,512]{4,3,2,1,0:T(8,128)(2,1)S(1)}, bf16[2,4,8,16,512]{4,3,2,1,0:T(8,128)(2,1)}, u32[]{:S(2)}) copy-start(bf16[2,4,8,16,512]{4,3,2,1,0:T(8,128)(2,1)} %get-tuple-element.19) | copy-start | bytes 3145732
  150.1 4.6 %slice-start.1 = ((s8[7077888]{0:T(1024)(128)(4,1)}), s8[2883584]{0:T(1024)(128)(4,1)S(1)}, s32[]{:S(2)}) async-start(s8[7077888]{0:T(1024)(128)(4,1)} %bitcast.302), calls=%async_computation.4 | async-start | bytes 5767168
  151.7 4.0 %copy-start.11 = (bf16[2,4,8,16,512]{4,3,2,1,0:T(8,128)(2,1)S(1)}, bf16[2,4,8,16,512]{4,3,2,1,0:T(8,128)(2,1)}, u32[]{:S(2)}) copy-start(bf16[2,4,8,16,512]{4,3,2,1,0:T(8,128)(2,1)} %get-tuple-element.18) | copy-start | bytes 3145732
  153.2 2.9 %copy-start.10 = (bf16[2,4,8,16,512]{4,3,2,1,0:T(8,128)(2,1)S(1)}, bf16[2,4,8,16,512]{4,3,2,1,0:T(8,128)(2,1)}, u32[]{:S(2)}) copy-start(bf16[2,4,8,16,512]{4,3,2,1,0:T(8,128)(2,1)} %get-tuple-element.17) | copy-start | bytes 3145732
  154.7 1.9 %copy-start.9 = (bf16[2,4,8,16,512]{4,3,2,1,0:T(8,128)(2,1)S(1)}, bf16[2,4,8,16,512]{4,3,2,1,0:T(8,128)(2,1)}, u32[]{:S(2)}) copy-start(bf16[2,4,8,16,512]{4,3,2,1,0:T(8,128)(2,1)} %get-tuple-element.16) | copy-start | bytes 3145732
  155.2 1.8 %copy-start.8 = (bf16[2,4,8,16,512]{4,3,2,1,0:T(8,128)(2,1)S(1)}, bf16[2,4,8,16,512]{4,3,2,1,0:T(8,128)(2,1)}, u32[]{:S(2)}) copy-start(bf16[2,4,8,16,512]{4,3,2,1,0:T(8,128)(2,1)} %get-tuple-element.15) | copy-start | bytes 3145732
  155.6 1.8 %copy-start.7 = (bf16[2,4,8,16,512]{4,3,2,1,0:T(8,128)(2,1)S(1)}, bf16[2,4,8,16,512]{4,3,2,1,0:T(8,128)(2,1)}, u32[]{:S(2)}) copy-start(bf16[2,4,8,16,512]{4,3,2,1,0:T(8,128)(2,1)} %get-tuple-element.14) | copy-start | bytes 3145732
  156.1 1.8 %copy-start.6 = (bf16[2,4,8,16,512]{4,3,2,1,0:T(8,128)(2,1)S(1)}, bf16[2,4,8,16,512]{4,3,2,1,0:T(8,128)(2,1)}, u32[]{:S(2)}) copy-start(bf16[2,4,8,16,512]{4,3,2,1,0:T(8,128)(2,1)} %get-tuple-element.13) | copy-start | bytes 3145732
  156.5 1.8 %copy-start.5 = (bf16[2,4,8,16,512]{4,3,2,1,0:T(8,128)(2,1)S(1)}, bf16[2,4,8,16,512]{4,3,2,1,0:T(8,128)(2,1)}, u32[]{:S(2)}) copy-start(bf16[2,4,8,16,512]{4,3,2,1,0:T(8,128)(2,1)} %get-tuple-element.12) | copy-start | bytes 3145732
  157.4 1.8 %copy-start.4 = (bf16[2,4,8,16,512]{4,3,2,1,0:T(8,128)(2,1)S(1)}, bf16[2,4,8,16,512]{4,3,2,1,0:T(8,128)(2,1)}, u32[]{:S(2)}) copy-start(bf16[2,4,8,16,512]{4,3,2,1,0:T(8,128)(2,1)} %get-tuple-element.10) | copy-start | bytes 3145732
  157.9 1.8 %copy-start.3 = (bf16[2,4,8,16,512]{4,3,2,1,0:T(8,128)(2,1)S(1)}, bf16[2,4,8,16,512]{4,3,2,1,0:T(8,128)(2,1)}, u32[]{:S(2)}) copy-start(bf16[2,4,8,16,512]{4,3,2,1,0:T(8,128)(2,1)} %get-tuple-element.9) | copy-start | bytes 3145732
  158.8 1.8 %copy-start.21 = (f32[256]{0:T(256)S(1)}, f32[256]{0:T(256)}, u32[]{:S(2)}) copy-start(f32[256]{0:T(256)} %param.25) | copy-start | bytes 3076
  159.3 2.6 %copy-start.1 = (bf16[2,4,4,8,2560]{4,3,2,1,0:T(8,128)(2,1)S(1)}, bf16[2,4,4,8,2560]{4,3,2,1,0:T(8,128)(2,1)}, u32[]{:S(2)}) copy-start(bf16[2,4,4,8,2560]{4,3,2,1,0:T(8,128)(2,1)} %param.13) | copy-start | bytes 3932164
Sparse Core Ops, SparseCore 0:
  11.7 23.4 all-reduce.4
  74.2 44.4 all-gather.4
Sparse Core Ops, SparseCore 1:
  13.5 33.9 all-gather.2
where the time goes:
time: 170 us; the launch traced here: 169 us
  waiting for transfers between devices  47.7 us (28%)
  matrix products  39.7 us (23%)
  blocking collectives  29.3 us (17%)
  local copies, waits for them, and re-layouts  22.8 us (13%)
  between operations  16.4 us (10%)
  starting transfers between devices  7.87 us (5%)
  other arithmetic  5.44 us (3%)
    all_gather x1, waiting for transfers between devices, shards(): lax.all_gather(m_pad, 'section', axis=4, tiled=True)  43.2 us
    dot_general x54, matrix products, tap_sum(): jnp.dot(tap, weight[a, b, e], preferred_element_type=jnp.float32)  35.2 us
    all_gather x1, blocking collectives, shards(): lax.all_gather(lat_cache, 'dec', axis=0, tiled=True)  22.1 us
    slice x4, local copies, waits for them, and re-layouts, tap_sum(): tap = padded[:, a:a + frames, b:b + rows, e:e + cols].reshape(-1, cin)  16 us
    psum x1, blocking collectives, shards(): lax.psum((jnp.sum(grouped, (1, 3)), jnp.sum(grouped * grouped, (1, 3))),...  7.16 us
    ppermute x2, starting transfers between devices, extended(): lax.ppermute(lax.slice_in_dim(block, block.shape[dim] - width, None, axis...  4.98 us
  transfers between devices with their start and end apart: 7, of which 3 were waited for; matrix products, arithmetic and copies ran while one was open for 10% of the time, Pallas kernels for 0%

commit v1 on v0

v1 whole, which is shorter than its diff:
```python
import functools

import jax
import jax.numpy as jnp
from jax import lax
from jax.experimental import pallas as pl
from jax.experimental.pallas import tpu as pltpu
from jax.sharding import PartitionSpec as P

CZ = 16
GROUP = 16
MESH = pl.DeviceIdType.MESH
F32 = jnp.float32
BF16 = jnp.bfloat16


def shifted(flat, step):
    n = flat.shape[0]
    j = lax.broadcasted_iota(jnp.int32, flat.shape, 0) % 8
    if step < 0:
        return jnp.where(j == 0, 0.0, pltpu.roll(flat, 1, 0))
    return jnp.where(j == 7, 0.0, pltpu.roll(flat, n - 1, 0))


def kernel(
    n_dec,
    n_row,
    hidden,
    head_t,
    head_bias,
    lat,
    mid,
    moves,
    span,
    cw,
    cb,
    gain,
    gbias,
    midw,
    midb,
    decoded,
    new_lat,
    new_mid,
    hid_v,
    midw_v,
    part,
    part_x,
    part_h,
    lat_all,
    lat_own,
    lat_h,
    cw_all,
    par_all,
    wide,
    z,
    h1,
    stats,
    stats_in,
    gm,
    pm,
    mb,
    acc,
    local_sem,
    lat_s,
    lat_r,
    mid_s,
    mid_r,
    w_s,
    w_r,
    part_s,
    part_r,
    lh_s,
    lh_r,
    st_s,
    st_r,
    pm_s,
    pm_r,
):
    s = lax.axis_index("section")
    d = lax.axis_index("dec")
    r = lax.axis_index("row")
    o = 1 - s
    lanes = pl.ds(pl.multiple_of(s * 256, 256), 256)
    olanes = pl.ds(pl.multiple_of(o * 256, 256), 256)
    has_up = r > 0
    has_down = r < n_row - 1

    barrier = pltpu.get_barrier_semaphore()

    def greet(dev):
        pl.semaphore_signal(barrier, inc=1, device_id=dev, device_id_type=MESH)

    greet((o, d, r))
    for k in range(1, n_dec):
        greet((s, lax.rem(d + k, n_dec), r))
    for k in range(1, n_row):
        greet((s, d, lax.rem(r + k, n_row)))
        greet((o, d, lax.rem(r + k, n_row)))

    load_hidden = pltpu.make_async_copy(hidden, hid_v, local_sem.at[0])
    load_hidden.start()
    own_mid = pltpu.make_async_copy(mid, gm.at[pl.ds(2 * d, 2)], local_sem.at[1])
    own_mid.start()
    load_w = pltpu.make_async_copy(midw, midw_v, local_sem.at[2])
    load_w.start()

    pl.semaphore_wait(barrier, 1 + (n_dec - 1) + 2 * (n_row - 1))

    def remote(src, dst, ssem, rsem, dev):
        return pltpu.make_async_remote_copy(
            src_ref=src, dst_ref=dst, send_sem=ssem, recv_sem=rsem, device_id=dev, device_id_type=MESH
        )

    def lat_copy(k, origin):
        return remote(
            lat, lat_all.at[pl.ds(2 * origin, 2)], lat_s.at[k - 1], lat_r.at[k - 1],
            (s, lax.rem(d + k, n_dec), r),
        )

    def mid_copy(k, origin):
        return remote(
            mid, gm.at[pl.ds(2 * origin, 2)], mid_s.at[k - 1], mid_r.at[k - 1],
            (s, lax.rem(d + k, n_dec), r),
        )

    for k in range(1, n_dec):
        lat_copy(k, d).start()

    cw_copy = remote(cw, cw_all.at[:, :, lanes], w_s.at[0], w_r.at[0], (o, d, r))
    cw_copy.start()
    par_copies = [
        remote(ref, par_all.at[n, :, lanes], w_s.at[n + 1], w_r.at[n + 1], (o, d, r))
        for n, ref in enumerate((cb, gain, gbias))
    ]
    for c in par_copies:
        c.start()
    for k in range(1, n_dec):
        mid_copy(k, d).start()

    load_hidden.wait()
    head = lax.dot_general(
        hid_v[...], head_t[...], (((1,), (1,)), ((), ())), preferred_element_type=F32
    )
    head = head.reshape(2, 4, 4, 8, 128)
    lane = lax.broadcasted_iota(jnp.int32, (4, 8, 128), 2)
    for t in range(2):
        for st in range(2):
            high = pltpu.roll(head[st, t + 2].reshape(32, 128), 64, 1).reshape(4, 8, 128)
            part[t, :, pl.ds(8 * st, 8), :] = jnp.where(lane < 64, head[st, t], high)

    def part_copies():
        full = remote(part, part_x, part_s.at[0], part_r.at[0], (o, d, r))
        up = [
            remote(part.at[:, 0], part_h.at[1, n], part_s.at[1 + n], part_r.at[1 + n], (dev, d, r - 1))
            for n, dev in enumerate((s, o))
        ]
        down = [
            remote(part.at[:, 3], part_h.at[0, n], part_s.at[3 + n], part_r.at[3 + n], (dev, d, r + 1))
            for n, dev in enumerate((s, o))
        ]
        return full, up, down

    full, up, down = part_copies()

    @pl.when(has_up)
    def _():
        for c in up:
            c.start()

    @pl.when(has_down)
    def _():
        for c in down:
            c.start()

    full.start()

    lat_all[pl.ds(2 * d, 2)] = lat[...]
    cw_all[:, :, lanes] = cw[...]
    for n, ref in enumerate((cb, gain, gbias)):
        par_all[n, :, lanes] = ref[...]

    for k in range(1, n_dec):
        lat_copy(k, lax.rem(d + n_dec - k, n_dec)).wait_recv()
    for st in range(2):
        live = (span[st] > 0).astype(F32)
        x = lat_all[moves[2 * d + st]].astype(F32) * live
        lat_own[:, pl.ds(8 * st, 8), :] = x.reshape(4, 8, 128)
    lat_edge_up = remote(lat_own.at[0], lat_h.at[1], lh_s.at[0], lh_r.at[0], (s, d, r - 1))
    lat_edge_down = remote(lat_own.at[3], lat_h.at[0], lh_s.at[1], lh_r.at[1], (s, d, r + 1))

    @pl.when(has_up)
    def _():
        lat_edge_up.start()

    @pl.when(has_down)
    def _():
        lat_edge_down.start()

    remote(cw, cw_all.at[:, :, olanes], w_s.at[0], w_r.at[0], (o, d, r)).wait_recv()
    for n, ref in enumerate((cb, gain, gbias)):
        remote(ref, par_all.at[n, :, olanes], w_s.at[n + 1], w_r.at[n + 1], (o, d, r)).wait_recv()
    zero_slab = jnp.zeros((CZ, 512), BF16)

    def build(a, carry):
        for pp in range(2):
            for qq in range(2):
                for di in range(2):
                    for dj in range(2):
                        for p in range(2):
                            for q in range(2):
                                b = 2 * di + p - 1 + pp
                                e = 2 * dj + q - 1 + qq
                                row = di * 128 + dj * 64 + p * 32 + q * 16
                                if 0 <= b < 3 and 0 <= e < 3:
                                    slab = cw_all[a * 9 + b * 3 + e]
                                else:
                                    slab = zero_slab
                                wide[pp * 2 + qq, a, pl.ds(row, 16), :] = slab
        return carry

    lax.fori_loop(0, 3, build, 0)

    full.wait_recv()

    @pl.when(has_up)
    def _():
        for c in down:
            c.wait_recv()
        lat_edge_down.wait_recv()

    @pl.when(has_down)
    def _():
        for c in up:
            c.wait_recv()
        lat_edge_up.wait_recv()

    bias = head_bias[...]

    def place(low, base, step, packed):
        count = packed.shape[0]
        flat = packed.astype(BF16).astype(F32).reshape(count * 16, 128)
        lane = lax.broadcasted_iota(jnp.int32, flat.shape, 1) < 64
        turn = pltpu.roll(flat, 64, 1)
        before = shifted(flat, -1)
        after = shifted(flat, 1)
        turn_before = pltpu.roll(before, 64, 1)
        turn_after = pltpu.roll(after, 64, 1)
        for q, frame, left, right in (
            (0, base, before, turn),
            (0, base + step, turn_before, flat),
            (1, base, flat, turn_after),
            (1, base + step, turn, after),
        ):
            z[q, frame, pl.ds(low, count)] = (
                jnp.where(lane, left, right).astype(BF16).reshape(count, 16, 128)
            )

    up_live = has_up.astype(F32)
    down_live = has_down.astype(F32)

    @pl.when(jnp.logical_not(has_up))
    def _():
        part_h[0] = jnp.zeros((2, 2, 16, 128), F32)
        lat_h[0] = jnp.zeros((16, 128), F32)

    @pl.when(jnp.logical_not(has_down))
    def _():
        part_h[1] = jnp.zeros((2, 2, 16, 128), F32)
        lat_h[1] = jnp.zeros((16, 128), F32)

    for t in range(2):
        own = part[t] + part_x[t] + bias
        new_lat[t] = own.astype(BF16)
        place(1, 2 + t, 2, own)
        place(0, 2 + t, 2, ((part_h[0, 0, t] + part_h[0, 1, t] + bias) * up_live)[None])
        place(5, 2 + t, 2, ((part_h[1, 0, t] + part_h[1, 1, t] + bias) * down_live)[None])
    place(1, 0, 1, lat_own[...])
    place(0, 0, 1, lat_h[0][None])
    place(5, 0, 1, lat_h[1][None])

    total = jnp.zeros((16, 512), F32)
    square = jnp.zeros((16, 512), F32)
    conv_bias = par_all[0]
    for pp in range(2):
        for qq in range(2):
            out = jnp.zeros((320, 512), F32)
            for a in range(3):
                lhs = jnp.concatenate(
                    [z[qq, a : a + 4, di : di + 5].reshape(320, 128) for di in range(2)], axis=1
                )
                out = out + jnp.dot(lhs, wide[pp * 2 + qq, a], preferred_element_type=F32)
            first = (out + conv_bias).astype(BF16)
            h1[pp * 2 + qq] = first.reshape(4, 5, 16, 512)
            mine = first.astype(F32).reshape(4, 5, 16, 512)[:, pp : pp + 4].reshape(16, 16, 512)
            total = total + jnp.sum(mine, axis=0)
            square = square + jnp.sum(mine * mine, axis=0)
    stats[...] = jnp.concatenate(
        [
            jnp.sum(total[0:8], axis=0, keepdims=True),
            jnp.sum(total[8:16], axis=0, keepdims=True),
            jnp.sum(square[0:8], axis=0, keepdims=True),
            jnp.sum(square[8:16], axis=0, keepdims=True),
            jnp.zeros((4, 512), F32),
        ],
        axis=0,
    )
    stat_copies = [
        remote(stats, stats_in.at[k - 1], st_s.at[k - 1], st_r.at[k - 1], (s, d, lax.rem(r + k, n_row)))
        for k in range(1, n_row)
    ]
    for c in stat_copies:
        c.start()
    for c in stat_copies:
        c.wait_recv()
    sums = stats[...]
    for k in range(1, n_row):
        sums = sums + stats_in[k - 1]
    lane8 = lax.broadcasted_iota(jnp.int32, (8, 512), 1)
    for k in (1, 2, 4, 8):
        other = jnp.where((lane8 & k) > 0, pltpu.roll(sums, k, 1), pltpu.roll(sums, 512 - k, 1))
        sums = sums + other
    sums = sums / (4 * 8 * 16 * GROUP * n_row)
    gv = sums[2:4] - sums[0:2] * sums[0:2]
    scale = lax.rsqrt(gv + 1e-5) * par_all[1]
    shift = par_all[2]

    def spread(v):
        return jnp.concatenate(
            [jnp.broadcast_to(v[0:1], (8, 512)), jnp.broadcast_to(v[1:2], (8, 512))], axis=0
        )

    mean16 = spread(sums[0:2])
    scale16 = spread(scale)

    def activate(t, carry):
        for pp in range(2):
            for qq in range(2):
                v = (h1[pp * 2 + qq, t].astype(F32) - mean16) * scale16 + shift
                v = v * (0.5 * jnp.tanh(0.5 * v) + 0.5)
                edge = lax.broadcasted_iota(jnp.int32, (5, 16, 512), 0)
                if pp == 1:
                    v = jnp.where((edge == 0) & jnp.logical_not(has_up), 0.0, v)
                else:
                    v = jnp.where((edge == 4) & jnp.logical_not(has_down), 0.0, v)
                v = v.astype(BF16)
                mb[pp, qq, t + 2] = v
                moved = shifted(v.astype(F32).reshape(80, 512), -1 if qq == 1 else 1)
                mb[pp, 2 if qq == 1 else 3, t + 2] = moved.astype(BF16).reshape(5, 16, 512)
        return carry

    lax.fori_loop(0, 4, activate, 0)

    acc[...] = jnp.zeros_like(acc)

    def conv(k, pairs):
        b = k // 3
        e = k % 3
        for a, t0, nt in pairs:
            pieces = []
            for pp in range(2):
                src = (b + 1) % 2 if pp == 0 else b % 2
                off = b // 2 if pp == 0 else (b + 1) // 2
                for qq in range(2):
                    var = (e + 2) % 3 if qq == 0 else e + e // 2
                    pieces.append(
                        mb[src, var, t0 + a : t0 + a + nt, pl.ds(off, 4)].reshape(nt * 64, 512)
                    )
            lhs = jnp.concatenate(pieces, axis=0)
            got = jnp.dot(lhs, midw_v[a * 9 + k], preferred_element_type=F32)
            acc[:, t0 : t0 + nt] += got.reshape(4, nt, 64, 256)

    load_w.wait()

    def tap_late(k, carry):
        conv(k, ((2, 0, 4),))
        return carry

    lax.fori_loop(0, 9, tap_late, 0)

    own_mid.wait()
    for k in range(1, n_dec):
        mid_copy(k, lax.rem(d + n_dec - k, n_dec)).wait_recv()
    zero_row = jnp.zeros((2, 32, 512), BF16)

    @pl.when(jnp.logical_not(has_up))
    def _():
        pm[:, 0] = zero_row

    @pl.when(jnp.logical_not(has_down))
    def _():
        pm[:, 9] = zero_row

    for st in range(2):
        live = (span[st] > 0).astype(BF16)
        pm[:, 1:9, pl.ds(16 * st, 16), lanes] = gm[moves[2 * d + st]] * live

    pm_full = remote(
        pm.at[:, 1:9, :, lanes], pm.at[:, 1:9, :, lanes], pm_s.at[0], pm_r.at[0], (o, d, r)
    )
    pm_up = [
        remote(pm.at[:, 1, :, lanes], pm.at[:, 9, :, lanes], pm_s.at[1 + n], pm_r.at[1 + n], (dev, d, r - 1))
        for n, dev in enumerate((s, o))
    ]
    pm_down = [
        remote(pm.at[:, 8, :, lanes], pm.at[:, 0, :, lanes], pm_s.at[3 + n], pm_r.at[3 + n], (dev, d, r + 1))
        for n, dev in enumerate((s, o))
    ]
    pm_full.start()

    @pl.when(has_up)
    def _():
        for c in pm_up:
            c.start()

    @pl.when(has_down)
    def _():
        for c in pm_down:
            c.start()

    def tap_mid(k, carry):
        conv(k, ((1, 1, 3), (0, 2, 2)))
        return carry

    lax.fori_loop(0, 9, tap_mid, 0)

    def blend(rows, cols, offs):
        return offs

    ro = lax.broadcasted_iota(jnp.int32, (64, 32), 0)
    co = lax.broadcasted_iota(jnp.int32, (64, 32), 1)
    v4 = ro // 16
    j2 = 2 * (ro % 8)
    col = jnp.where(v4 == 0, j2, jnp.where(v4 == 1, j2 + 1, jnp.where(v4 == 2, j2 - 1, j2 + 2)))
    fits = (col >= 0) & (col < 16) & (co == (ro // 8) % 2 * 16 + col)
    deal = jnp.where(fits, 1.0, 0.0).astype(BF16)

    ro = lax.broadcasted_iota(jnp.int32, (32, 32), 0)
    co = lax.broadcasted_iota(jnp.int32, (32, 32), 1)
    weave = jnp.where(co == (ro % 2) * 16 + (ro // 16) * 8 + (ro % 16) // 2, 1.0, 0.0).astype(BF16)

    def keep_mid(t, carry):
        for pp in range(2):
            for i in range(4):
                y = jnp.concatenate(
                    [mb[pp, 0, t + 4, i + pp, :, lanes], mb[pp, 1, t + 4, i + pp, :, lanes]], axis=0
                )
                y = jnp.dot(weave, y, preferred_element_type=F32).astype(BF16)
                new_mid[0, t, 2 * i + pp] = y[0:16]
                new_mid[1, t, 2 * i + pp] = y[16:32]
        return carry

    lax.fori_loop(0, 2, keep_mid, 0)

    pm_full_in = remote(
        pm.at[:, 1:9, :, olanes], pm.at[:, 1:9, :, olanes], pm_s.at[0], pm_r.at[0], (o, d, r)
    )
    pm_full_in.wait_recv()

    @pl.when(has_up)
    def _():
        for n, c in enumerate((lanes, olanes)):
            remote(
                pm.at[:, 8, :, c], pm.at[:, 0, :, c], pm_s.at[3 + n], pm_r.at[3 + n], (s, d, r - 1)
            ).wait_recv()

    @pl.when(has_down)
    def _():
        for n, c in enumerate((lanes, olanes)):
            remote(
                pm.at[:, 1, :, c], pm.at[:, 9, :, c], pm_s.at[1 + n], pm_r.at[1 + n], (s, d, r + 1)
            ).wait_recv()

    def unfold(f, carry):
        for row in range(10):
            y = jnp.dot(deal, pm[f, row], preferred_element_type=F32).astype(BF16)
            for v in range(4):
                mb[(row + 1) % 2, v, f, row // 2] = y[16 * v : 16 * v + 16]
        return carry

    lax.fori_loop(0, 2, unfold, 0)

    def tap_early(k, carry):
        conv(k, ((1, 0, 1), (0, 0, 2)))
        return carry

    lax.fori_loop(0, 9, tap_early, 0)

    def finish(t, carry):
        for pp in range(2):
            for i in range(4):
                y = jnp.concatenate(
                    [
                        h1[pp * 2 + qq, t, i + pp, :, lanes].astype(F32)
                        + acc[pp * 2 + qq, t, pl.ds(16 * i, 16)]
                        + midb[...]
                        for qq in range(2)
                    ],
                    axis=0,
                ).astype(BF16)
                y = jnp.dot(weave, y, preferred_element_type=F32).astype(BF16)
                decoded[0, t, 2 * i + pp] = y[0:16]
                decoded[1, t, 2 * i + pp] = y[16:32]
        return carry

    lax.fori_loop(0, 4, finish, 0)

    for k in range(1, n_dec):
        lat_copy(k, d).wait_send()
        mid_copy(k, d).wait_send()
    cw_copy.wait_send()
    for c in par_copies + stat_copies + [full, pm_full]:
        c.wait_send()

    @pl.when(has_up)
    def _():
        for c in up + pm_up + [lat_edge_up]:
            c.wait_send()

    @pl.when(has_down)
    def _():
        for c in down + pm_down + [lat_edge_down]:
            c.wait_send()


def shards(
    n_dec,
    n_row,
    hidden,
    head_weight,
    head_bias,
    lat_cache,
    mid_cache,
    moves,
    span_index,
    conv_in_weight,
    conv_in_bias,
    gn_gain,
    gn_bias,
    mid_weight,
    mid_bias,
):
    slots = n_dec * 2
    depth = hidden.shape[-1]
    head_t = jnp.pad(head_weight.T, ((0, 64), (0, 0)))
    bias = jnp.concatenate([head_bias, head_bias]).reshape(1, 128)
    lat = lat_cache.reshape(2, 2, 4, 2, 8, 2, CZ).transpose(0, 2, 4, 1, 3, 5, 6).reshape(2, 32, 128)
    vm = pl.BlockSpec(memory_space=pltpu.VMEM)
    sm = pl.BlockSpec(memory_space=pltpu.SMEM)
    hbm = pl.BlockSpec(memory_space=pl.ANY)
    dma = pltpu.SemaphoreType.DMA
    decoded, latent, new_mid = pl.pallas_call(
        functools.partial(kernel, n_dec, n_row),
        out_shape=(
            jax.ShapeDtypeStruct((2, 4, 8, 16, 256), BF16),
            jax.ShapeDtypeStruct((2, 4, 16, 128), BF16),
            jax.ShapeDtypeStruct((2, 2, 8, 16, 256), BF16),
        ),
        in_specs=[hbm, vm, vm, vm, hbm, sm, sm, vm, vm, vm, vm, hbm, vm],
        out_specs=(vm, vm, vm),
        scratch_shapes=[
            pltpu.VMEM((256, depth), BF16),
            pltpu.VMEM((27, 512, 256), BF16),
            pltpu.VMEM((2, 4, 16, 128), F32),
            pltpu.VMEM((2, 4, 16, 128), F32),
            pltpu.VMEM((2, 2, 2, 16, 128), F32),
            pltpu.VMEM((slots, 32, 128), BF16),
            pltpu.VMEM((4, 16, 128), F32),
            pltpu.VMEM((2, 16, 128), F32),
            pltpu.VMEM((27, CZ, 512), BF16),
            pltpu.VMEM((3, 1, 512), F32),
            pltpu.VMEM((4, 3, 256, 512), BF16),
            pltpu.VMEM((2, 6, 6, 16, 128), BF16),
            pltpu.VMEM((4, 4, 5, 16, 512), BF16),
            pltpu.VMEM((8, 512), F32),
            pltpu.VMEM((n_row - 1, 8, 512), F32),
            pltpu.VMEM((slots, 2, 8, 16, 256), BF16),
            pltpu.VMEM((2, 10, 32, 512), BF16),
            pltpu.VMEM((2, 4, 6, 5, 16, 512), BF16),
            pltpu.VMEM((4, 4, 64, 256), F32),
            dma((3,)),
            dma((n_dec - 1,)),
            dma((n_dec - 1,)),
            dma((n_dec - 1,)),
            dma((n_dec - 1,)),
            dma((4,)),
            dma((4,)),
            dma((5,)),
            dma((5,)),
            dma((2,)),
            dma((2,)),
            dma((n_row - 1,)),
            dma((n_row - 1,)),
            dma((5,)),
            dma((5,)),
        ],
        compiler_params=pltpu.CompilerParams(
            collective_id=0, has_side_effects=True, vmem_limit_bytes=56 * 1024 * 1024
        ),
        cost_estimate=pl.CostEstimate(
            flops=9_000_000_000, bytes_accessed=12_000_000, transcendentals=700_000
        ),
    )(
        hidden.reshape(256, depth),
        head_t,
        bias,
        lat,
        mid_cache,
        moves,
        span_index,
        conv_in_weight.reshape(27, CZ, 256),
        conv_in_bias.reshape(1, 256),
        gn_gain.reshape(1, 256),
        gn_bias.reshape(1, 256),
        mid_weight.reshape(27, 512, 256),
        mid_bias.reshape(1, 256),
    )
    kept = latent[..., 64:].reshape(2, 4, 2, 8, 2, 2, CZ)
    kept = kept.transpose(2, 0, 1, 4, 3, 5, 6).reshape(2, 2, 8, 16, CZ)
    return decoded, kept, new_mid


def solution(mesh):
    placed = (
        P("dec", None, "row", None, "section"),
        P("section", None),
        P(),
        P("dec", None, "row", None, None),
        P("dec", None, "row", None, "section"),
        P(),
        P("dec"),
        P(None, None, None, None, "section"),
        P("section"),
        P("section"),
        P("section"),
        P(None, None, None, None, "section"),
        P("section"),
    )
    return jax.shard_map(
        functools.partial(shards, mesh.shape["dec"], mesh.shape["row"]),
        mesh=mesh,
        in_specs=placed,
        out_specs=(
            P("dec", None, "row", None, "section"),
            P("dec", None, "row", None, None),
            P("dec", None, "row", None, "section"),
        ),
        check_vma=False,
    )
```

time: 170 us -> 58.3 us (0.34)
  the two profiles are of different devices: /device:TPU:0 before, /device:TPU:1 now
where the time goes in v1:
time: 58.3 us; the launch traced here: 58 us
  Pallas kernels  47.2 us (81%)
  local copies, waits for them, and re-layouts  8.84 us (15%)
  other arithmetic  1.32 us (2%)
  between operations  0.65 us (1%)
    pallas_call x1, Pallas kernels, shards(): pl.pallas_call(functools.partial(kernel, n_dec, n_row), out_shape=(jax.Sh...  47.2 us
    unnamed x2, local copies, waits for them, and re-layouts  3.54 us
    pad x1, local copies, waits for them, and re-layouts, shards(): head_t = jnp.pad(head_weight.T, ((0, 64), (0, 0)))  1.86 us
    reshape x2, local copies, waits for them, and re-layouts, shards(): lat_cache.reshape(2, 2, 4, 2, 8, 2, CZ).transpose(0, 2, 4, 1, 3, 5, 6)  1.74 us
    reshape x1, other arithmetic, shards(): bias = jnp.concatenate([head_bias, head_bias]).reshape(1, 128)  1.32 us

profile of v1, /device:TPU:1, one launch (start us, length us, event | category | flops | bytes accessed | tf_op | source)
XLA Modules:
  0.0 58.0 jit_solution(18431813213225353063)
XLA Ops:
  0.6 1.3 %maximum_bitcast_fusion.head_bias = f32[1,128]{1,0:T(1,128)} fusion(f32[64]{0:T(128)} %param.15), kind=kLoop, calls=%fused_computation.1 | loop fusion | flops 128 | bytes 768 | tf_op jit(solution)/shard_map/reshape | solution.py:545
  1.9 1.0 %copy.19 = bf16[2,2,4,2,8,2,16]{6,5,3,1,4,2,0:T(2,128)(2,1)S(1)} copy(bf16[2,2,4,2,8,2,16]{6,5,4,3,2,1,0:T(2,128)(2,1)} %bitcast.21) | data formatting | bytes 32768 | tf_op jit(solution)/shard_map/reshape | solution.py:546
  2.9 0.7 %reshape.45.lat = bf16[2,32,128]{2,1,0:T(8,128)(2,1)} reshape(bf16[2,4,8,2,2,2,16]{6,5,4,3,2,1,0:T(2,128)(2,1)S(1)} %bitcast.19) | data formatting | bytes 32768 | tf_op jit(solution)/shard_map/reshape | solution.py:546
  3.7 1.9 %pad.4.head_t = bf16[128,2560]{1,0:T(8,128)(2,1)} pad(bf16[64,2560]{1,0:T(8,128)(2,1)} %bitcast.20, bf16[]{:T(256)} %constant.2.clone.1), padding=0_64x0_0 | pad | bytes 983042 | tf_op jit(solution)/shard_map/jit(_pad)/pad | solution.py:544
  5.5 47.2 %shard_map.148 = (bf16[2,4,8,16,256]{4,3,2,1,0:T(8,128)(2,1)}, bf16[2,4,16,128]{3,2,1,0:T(8,128)(2,1)}, bf16[2,2,8,16,256]{4,3,2,1,0:T(8,128)(2,1)}) custom-call(bf16[256,2560]{1,0:T(8,128)(2,1)} %bitcast.24, bf16[128,2560]{1,0:T(8,128)(2,1)} %pad.4.head_t, f32[1,128]{1,0:T(1,128)} %maximum_bitcast_fusion.head_bias, bf16[2,32,128]{2,1,0:T(8,128)(2,1)} %reshape.45.lat, ...), custom_call_target="tpu_custom_call" | custom-call | flops 8999999488 | bytes 12000000 | tf_op jit(solution)/shard_map/pallas_call | solution.py:551
  52.7 0.8 %slice.3 = bf16[2,4,16,64]{3,2,1,0:T(8,128)(2,1)S(1)} slice(bf16[2,4,16,128]{3,2,1,0:T(8,128)(2,1)} %get-tuple-element.7), slice={[0:2], [0:4], [0:16], [64:128]} | slice | bytes 32768 | tf_op jit(solution)/shard_map/slice | solution.py:617
  53.6 0.1 reshape.52
  53.7 0.8 %copy.17 = bf16[2,2,4,2,8,2,16]{6,5,4,3,2,1,0:T(2,128)(2,1)} copy(bf16[2,2,4,2,8,2,16]{6,5,3,4,0,2,1:T(2,128)(2,1)S(1)} %bitcast.18) | data formatting | bytes 32768 | tf_op jit(solution)/shard_map/transpose | solution.py:618
  54.5 1.9 %copy.22 = bf16[2,4,8,16,256]{4,3,2,1,0:T(8,128)(2,1)} copy(bf16[2,4,8,16,256]{4,3,2,1,0:T(8,128)(2,1)} %get-tuple-element.12) | data formatting | bytes 1048576
  56.3 1.7 %copy.23 = bf16[2,2,8,16,256]{4,3,2,1,0:T(8,128)(2,1)} copy(bf16[2,2,8,16,256]{4,3,2,1,0:T(8,128)(2,1)} %get-tuple-element.14) | data formatting | bytes 524288

commit v2 on v1

--- a/solution.py
+++ b/solution.py
@@ -41,6 +41,7 @@
     decoded,
     new_lat,
     new_mid,
+    lat_pk,
     hid_v,
     midw_v,
     part,
@@ -56,7 +57,9 @@
     h1,
     stats,
     stats_in,
-    gm,
+    gm0,
+    gm1,
+    sel,
     pm,
     mb,
     acc,
@@ -65,6 +68,8 @@
     lat_r,
     mid_s,
     mid_r,
+    hop_s,
+    hop_r,
     w_s,
     w_r,
     part_s,
@@ -99,10 +104,41 @@
 
     load_hidden = pltpu.make_async_copy(hidden, hid_v, local_sem.at[0])
     load_hidden.start()
-    own_mid = pltpu.make_async_copy(mid, gm.at[pl.ds(2 * d, 2)], local_sem.at[1])
-    own_mid.start()
-    load_w = pltpu.make_async_copy(midw, midw_v, local_sem.at[2])
+    gm = (gm0, gm1)
+    own_mid = [
+        pltpu.make_async_copy(mid.at[:, f], gm[f].at[pl.ds(2 * d, 2)], local_sem.at[1 + f])
+        for f in range(2)
+    ]
+    for c in own_mid:
+        c.start()
+    load_w = pltpu.make_async_copy(midw, midw_v, local_sem.at[3])
     load_w.start()
+
+    ri = lax.broadcasted_iota(jnp.int32, (CZ, 128), 0)
+    ci = lax.broadcasted_iota(jnp.int32, (CZ, 128), 1)
+    tile = jnp.where(ci % CZ == ri, 1.0, 0.0).astype(BF16)
+    wide_lat = jnp.dot(lat[...].reshape(512, CZ), tile, preferred_element_type=F32)
+    wide_lat = wide_lat.reshape(2, 2, 4, 2, 16, 128)
+    lane6 = lax.broadcasted_iota(jnp.int32, (2, 4, 16, 128), 3) // 32
+    merged = jnp.where(
+        lane6 == 0,
+        wide_lat[:, 0, :, 0],
+        jnp.where(lane6 == 1, wide_lat[:, 0, :, 1], jnp.where(lane6 == 2, wide_lat[:, 1, :, 0], wide_lat[:, 1, :, 1])),
+    )
+    merged = merged.reshape(128, 128).astype(BF16)
+    ri = lax.broadcasted_iota(jnp.int32, (64, 128), 0)
+    ci = lax.broadcasted_iota(jnp.int32, (64, 128), 1)
+    halves = [
+        jnp.dot(
+            jnp.where(ci == ri // 8 * 16 + 2 * (ri % 8) + q, 1.0, 0.0).astype(BF16),
+            merged,
+            preferred_element_type=F32,
+        )
+        for q in range(2)
+    ]
+    lat_pk[...] = (
+        jnp.where(ci // 16 % 2 == 0, halves[0], halves[1]).astype(BF16).reshape(2, 32, 128)
+    )
 
     pl.semaphore_wait(barrier, 1 + (n_dec - 1) + 2 * (n_row - 1))
 
@@ -113,33 +149,92 @@
 
     def lat_copy(k, origin):
         return remote(
-            lat, lat_all.at[pl.ds(2 * origin, 2)], lat_s.at[k - 1], lat_r.at[k - 1],
+            lat_pk, lat_all.at[pl.ds(2 * origin, 2)], lat_s.at[k - 1], lat_r.at[k - 1],
             (s, lax.rem(d + k, n_dec), r),
         )
 
-    def mid_copy(k, origin):
+    def mid_copy(k, origin, f):
         return remote(
-            mid, gm.at[pl.ds(2 * origin, 2)], mid_s.at[k - 1], mid_r.at[k - 1],
+            mid.at[:, f], gm[f].at[pl.ds(2 * origin, 2)], mid_s.at[k - 1, f], mid_r.at[k - 1, f],
             (s, lax.rem(d + k, n_dec), r),
         )
 
+    line = n_dec == 4
+    inner = (d == 1) | (d == 2)
+    end = 3 * (d - 1)
+    near = 1 + d // 3
+
+    def end_copy(f):
+        return remote(
+            mid.at[:, f], gm[f].at[pl.ds(2 * d, 2)], hop_s.at[0, f], hop_r.at[0, f], (s, near, r)
+        )
+
+    def cross_copy(f):
+        return remote(
+            mid.at[:, f], gm[f].at[pl.ds(2 * d, 2)], hop_s.at[1, f], hop_r.at[1, f], (s, 3 - d, r)
+        )
+
+    def pass_copy(f):
+        slots = pl.ds(2 * end, 2)
+        return remote(
+            gm[f].at[slots], gm[f].at[slots], hop_s.at[2, f], hop_r.at[2, f], (s, 3 - d, r)
+        )
+
+    def pick_copy(f, target):
+        return remote(sel.at[f], sel.at[f], hop_s.at[3, f], hop_r.at[3, f], (s, target, r))
+
+    def pass_on(f):
+        if line:
+
+            @pl.when(inner)
+            def _():
+                end_copy(f).wait_recv()
+                pass_copy(f).start()
+
     for k in range(1, n_dec):
         lat_copy(k, d).start()
 
-    cw_copy = remote(cw, cw_all.at[:, :, lanes], w_s.at[0], w_r.at[0], (o, d, r))
+    half = lax.rem(r, 2)
+    half_lanes = pl.ds(pl.multiple_of(half * 128, 128), 128)
+    out_lanes = pl.ds(pl.multiple_of(s * 256 + half * 128, 128), 128)
+    in_lanes = pl.ds(pl.multiple_of(o * 256 + half * 128, 128), 128)
+    cw_copy = remote(
+        cw.at[:, :, half_lanes], cw_all.at[:, :, out_lanes], w_s.at[0], w_r.at[0], (o, d, r)
+    )
     cw_copy.start()
+    cw_pass = remote(
+        cw_all.at[:, :, in_lanes], cw_all.at[:, :, in_lanes], w_s.at[4], w_r.at[4],
+        (s, d, r + 1 - 2 * half),
+    )
     par_copies = [
         remote(ref, par_all.at[n, :, lanes], w_s.at[n + 1], w_r.at[n + 1], (o, d, r))
         for n, ref in enumerate((cb, gain, gbias))
     ]
     for c in par_copies:
         c.start()
-    for k in range(1, n_dec):
-        mid_copy(k, d).start()
+    if line:
+
+        @pl.when(inner)
+        def _():
+            for f in range(2):
+                cross_copy(f).start()
+
+        @pl.when(jnp.logical_not(inner))
+        def _():
+            for f in range(2):
+                end_copy(f).start()
+
+    else:
+        for k in range(1, n_dec):
+            for f in range(2):
+                mid_copy(k, d, f).start()
 
     load_hidden.wait()
     head = lax.dot_general(
-        hid_v[...], head_t[...], (((1,), (1,)), ((), ())), preferred_element_type=F32
+        hid_v[...],
+        jnp.concatenate([head_t[...], jnp.zeros_like(head_t)], axis=0),
+        (((1,), (1,)), ((), ())),
+        preferred_element_type=F32,
     )
     head = head.reshape(2, 4, 4, 8, 128)
     lane = lax.broadcasted_iota(jnp.int32, (4, 8, 128), 2)
@@ -174,7 +269,7 @@
 
     full.start()
 
-    lat_all[pl.ds(2 * d, 2)] = lat[...]
+    lat_all[pl.ds(2 * d, 2)] = lat_pk[...]
     cw_all[:, :, lanes] = cw[...]
     for n, ref in enumerate((cb, gain, gbias)):
         par_all[n, :, lanes] = ref[...]
@@ -196,9 +291,11 @@
     def _():
         lat_edge_down.start()
 
-    remote(cw, cw_all.at[:, :, olanes], w_s.at[0], w_r.at[0], (o, d, r)).wait_recv()
+    cw_copy.wait_recv()
+    cw_pass.start()
     for n, ref in enumerate((cb, gain, gbias)):
         remote(ref, par_all.at[n, :, olanes], w_s.at[n + 1], w_r.at[n + 1], (o, d, r)).wait_recv()
+    cw_pass.wait_recv()
     zero_slab = jnp.zeros((CZ, 512), BF16)
 
     def build(a, carry):
@@ -219,6 +316,7 @@
         return carry
 
     lax.fori_loop(0, 3, build, 0)
+    pass_on(0)
 
     full.wait_recv()
 
@@ -234,7 +332,7 @@
             c.wait_recv()
         lat_edge_up.wait_recv()
 
-    bias = head_bias[...]
+    bias = jnp.concatenate([head_bias[...], head_bias[...]], axis=1)
 
     def place(low, base, step, packed):
         count = packed.shape[0]
@@ -310,6 +408,7 @@
     ]
     for c in stat_copies:
         c.start()
+    pass_on(1)
     for c in stat_copies:
         c.wait_recv()
     sums = stats[...]
@@ -375,11 +474,6 @@
         conv(k, ((2, 0, 4),))
         return carry
 
-    lax.fori_loop(0, 9, tap_late, 0)
-
-    own_mid.wait()
-    for k in range(1, n_dec):
-        mid_copy(k, lax.rem(d + n_dec - k, n_dec)).wait_recv()
     zero_row = jnp.zeros((2, 32, 512), BF16)
 
     @pl.when(jnp.logical_not(has_up))
@@ -390,41 +484,77 @@
     def _():
         pm[:, 9] = zero_row
 
-    for st in range(2):
-        live = (span[st] > 0).astype(BF16)
-        pm[:, 1:9, pl.ds(16 * st, 16), lanes] = gm[moves[2 * d + st]] * live
-
-    pm_full = remote(
-        pm.at[:, 1:9, :, lanes], pm.at[:, 1:9, :, lanes], pm_s.at[0], pm_r.at[0], (o, d, r)
-    )
-    pm_up = [
-        remote(pm.at[:, 1, :, lanes], pm.at[:, 9, :, lanes], pm_s.at[1 + n], pm_r.at[1 + n], (dev, d, r - 1))
-        for n, dev in enumerate((s, o))
-    ]
-    pm_down = [
-        remote(pm.at[:, 8, :, lanes], pm.at[:, 0, :, lanes], pm_s.at[3 + n], pm_r.at[3 + n], (dev, d, r + 1))
-        for n, dev in enumerate((s, o))
-    ]
-    pm_full.start()
-
-    @pl.when(has_up)
-    def _():
-        for c in pm_up:
-            c.start()
-
-    @pl.when(has_down)
-    def _():
-        for c in pm_down:
-            c.start()
+    def pm_full(f):
+        block = pm.at[f, 1:9, :, lanes]
+        return remote(block, block, pm_s.at[f, 0], pm_r.at[f, 0], (o, d, r))
+
+    def pm_up(f):
+        return [
+            remote(pm.at[f, 1, :, lanes], pm.at[f, 9, :, lanes], pm_s.at[f, 1 + n], pm_r.at[f, 1 + n], (dev, d, r - 1))
+            for n, dev in enumerate((s, o))
+        ]
+
+    def pm_down(f):
+        return [
+            remote(pm.at[f, 8, :, lanes], pm.at[f, 0, :, lanes], pm_s.at[f, 3 + n], pm_r.at[f, 3 + n], (dev, d, r + 1))
+            for n, dev in enumerate((s, o))
+        ]
+
+    def share(f, pick):
+        for st in range(2):
+            live = (span[st] > 0).astype(BF16)
+            pm[f, 1:9, pl.ds(16 * st, 16), lanes] = pick(st) * live
+        pm_full(f).start()
+
+        @pl.when(has_up)
+        def _():
+            for c in pm_up(f):
+                c.start()
+
+        @pl.when(has_down)
+        def _():
+            for c in pm_down(f):
+                c.start()
+
+    def share_inner(f):
+        if line:
+
+            @pl.when(inner)
+            def _():
+                own_mid[f].wait()
+                cross_copy(f).wait_recv()
+                pass_copy(f).wait_recv()
+                for st in range(2):
+                    sel[f, :, pl.ds(16 * st, 16), :] = gm[f][moves[2 * end + st]]
+                pick_copy(f, end).start()
+                share(f, lambda st: gm[f][moves[2 * d + st]])
+
+    def share_end(f):
+        if line:
+
+            @pl.when(jnp.logical_not(inner))
+            def _():
+                pick_copy(f, near).wait_recv()
+                share(f, lambda st: sel[f, :, pl.ds(16 * st, 16), :])
+
+        else:
+            own_mid[f].wait()
+            for k in range(1, n_dec):
+                mid_copy(k, lax.rem(d + n_dec - k, n_dec), f).wait_recv()
+            share(f, lambda st: gm[f][moves[2 * d + st]])
+
+    share_inner(0)
+    lax.fori_loop(0, 4, tap_late, 0)
+    share_inner(1)
+    lax.fori_loop(4, 9, tap_late, 0)
+    share_end(0)
+    share_end(1)
 
     def tap_mid(k, carry):
         conv(k, ((1, 1, 3), (0, 2, 2)))
         return carry
 
     lax.fori_loop(0, 9, tap_mid, 0)
-
-    def blend(rows, cols, offs):
-        return offs
 
     ro = lax.broadcasted_iota(jnp.int32, (64, 32), 0)
     co = lax.broadcasted_iota(jnp.int32, (64, 32), 1)
@@ -434,41 +564,23 @@
     fits = (col >= 0) & (col < 16) & (co == (ro // 8) % 2 * 16 + col)
     deal = jnp.where(fits, 1.0, 0.0).astype(BF16)
 
-    ro = lax.broadcasted_iota(jnp.int32, (32, 32), 0)
-    co = lax.broadcasted_iota(jnp.int32, (32, 32), 1)
-    weave = jnp.where(co == (ro % 2) * 16 + (ro // 16) * 8 + (ro % 16) // 2, 1.0, 0.0).astype(BF16)
-
-    def keep_mid(t, carry):
+    for t in range(2):
         for pp in range(2):
-            for i in range(4):
-                y = jnp.concatenate(
-                    [mb[pp, 0, t + 4, i + pp, :, lanes], mb[pp, 1, t + 4, i + pp, :, lanes]], axis=0
-                )
-                y = jnp.dot(weave, y, preferred_element_type=F32).astype(BF16)
-                new_mid[0, t, 2 * i + pp] = y[0:16]
-                new_mid[1, t, 2 * i + pp] = y[16:32]
-        return carry
-
-    lax.fori_loop(0, 2, keep_mid, 0)
-
-    pm_full_in = remote(
-        pm.at[:, 1:9, :, olanes], pm.at[:, 1:9, :, olanes], pm_s.at[0], pm_r.at[0], (o, d, r)
-    )
-    pm_full_in.wait_recv()
-
-    @pl.when(has_up)
-    def _():
-        for n, c in enumerate((lanes, olanes)):
-            remote(
-                pm.at[:, 8, :, c], pm.at[:, 0, :, c], pm_s.at[3 + n], pm_r.at[3 + n], (s, d, r - 1)
-            ).wait_recv()
-
-    @pl.when(has_down)
-    def _():
-        for n, c in enumerate((lanes, olanes)):
-            remote(
-                pm.at[:, 1, :, c], pm.at[:, 9, :, c], pm_s.at[1 + n], pm_r.at[1 + n], (s, d, r + 1)
-            ).wait_recv()
+            for qq in range(2):
+                new_mid[t, pp, :, pl.ds(16 * qq, 16), :] = mb[pp, qq, t + 4, pp : pp + 4, :, lanes]
+
+    for f in range(2):
+        pm_full(f).wait_recv()
+
+        @pl.when(has_up)
+        def _():
+            for c in pm_down(f):
+                c.wait_recv()
+
+        @pl.when(has_down)
+        def _():
+            for c in pm_up(f):
+                c.wait_recv()
 
     def unfold(f, carry):
         for row in range(10):
@@ -487,39 +599,92 @@
 
     def finish(t, carry):
         for pp in range(2):
-            for i in range(4):
-                y = jnp.concatenate(
-                    [
-                        h1[pp * 2 + qq, t, i + pp, :, lanes].astype(F32)
-                        + acc[pp * 2 + qq, t, pl.ds(16 * i, 16)]
-                        + midb[...]
-                        for qq in range(2)
-                    ],
-                    axis=0,
-                ).astype(BF16)
-                y = jnp.dot(weave, y, preferred_element_type=F32).astype(BF16)
-                decoded[0, t, 2 * i + pp] = y[0:16]
-                decoded[1, t, 2 * i + pp] = y[16:32]
+            for qq in range(2):
+                y = (
+                    h1[pp * 2 + qq, t, pp : pp + 4, :, lanes].astype(F32)
+                    + acc[pp * 2 + qq, t].reshape(4, 16, 256)
+                    + midb[...]
+                )
+                decoded[t, pp, :, pl.ds(16 * qq, 16), :] = y.astype(BF16)
         return carry
 
     lax.fori_loop(0, 4, finish, 0)
 
     for k in range(1, n_dec):
         lat_copy(k, d).wait_send()
-        mid_copy(k, d).wait_send()
-    cw_copy.wait_send()
-    for c in par_copies + stat_copies + [full, pm_full]:
+    for c in par_copies + stat_copies + [full, cw_copy, cw_pass, pm_full(0), pm_full(1)]:
         c.wait_send()
+    if line:
+
+        @pl.when(inner)
+        def _():
+            for f in range(2):
+                cross_copy(f).wait_send()
+                pass_copy(f).wait_send()
+                pick_copy(f, end).wait_send()
+
+        @pl.when(jnp.logical_not(inner))
+        def _():
+            for f in range(2):
+                end_copy(f).wait_send()
+                own_mid[f].wait()
+
+    else:
+        for k in range(1, n_dec):
+            for f in range(2):
+                mid_copy(k, d, f).wait_send()
 
     @pl.when(has_up)
     def _():
-        for c in up + pm_up + [lat_edge_up]:
+        for c in up + pm_up(0) + pm_up(1) + [lat_edge_up]:
             c.wait_send()
 
     @pl.when(has_down)
     def _():
-        for c in down + pm_down + [lat_edge_down]:
+        for c in down + pm_down(0) + pm_down(1) + [lat_edge_down]:
             c.wait_send()
+
+
+def weave_kernel(decoded, new_lat, new_mid, decoded_out, new_lat_out, new_mid_out):
+    ro = lax.broadcasted_iota(jnp.int32, (32, 32), 0)
+    co = lax.broadcasted_iota(jnp.int32, (32, 32), 1)
+    weave = jnp.where(co == (ro % 2) * 16 + (ro // 16) * 8 + (ro % 16) // 2, 1.0, 0.0).astype(BF16)
+
+    def spread(source, target, t):
+        for pp in range(2):
+            for i in range(4):
+                y = jnp.dot(weave, source[t, pp, i], preferred_element_type=F32).astype(BF16)
+                target[0, t, 2 * i + pp] = y[0:16]
+                target[1, t, 2 * i + pp] = y[16:32]
+
+    for t in range(4):
+        spread(decoded, decoded_out, t)
+    for t in range(2):
+        spread(new_mid, new_mid_out, t)
+
+    patches = new_lat[...].reshape(128, 128)
+    ro = lax.broadcasted_iota(jnp.int32, (256, 128), 0)
+    co = lax.broadcasted_iota(jnp.int32, (256, 128), 1)
+    grown = [
+        jnp.dot(
+            jnp.where((co == ro // 16 * 8 + ro % 16 // 2) & (ro % 2 == q), 1.0, 0.0).astype(BF16),
+            patches,
+            preferred_element_type=F32,
+        )
+        for q in range(2)
+    ]
+    grown = jnp.where(co // 16 % 2 == 0, grown[0], grown[1])
+    ro = lax.broadcasted_iota(jnp.int32, (128, CZ), 0)
+    for p in range(2):
+        fold = (ro // 32 == 2 + p) & (ro % CZ == lax.broadcasted_iota(jnp.int32, (128, CZ), 1))
+        y = jnp.dot(
+            grown.astype(BF16), jnp.where(fold, 1.0, 0.0).astype(BF16), preferred_element_type=F32
+        ).astype(BF16)
+        for t in range(2):
+            for i in range(4):
+                for st in range(2):
+                    row = ((t * 4 + i) * 2 + st) * 16
+                    new_lat_out[st, t, 2 * i + p] = y[row : row + 16]
 
 
 def shards(
@@ -541,23 +706,21 @@
 ):
     slots = n_dec * 2
     depth = hidden.shape[-1]
-    head_t = jnp.pad(head_weight.T, ((0, 64), (0, 0)))
-    bias = jnp.concatenate([head_bias, head_bias]).reshape(1, 128)
-    lat = lat_cache.reshape(2, 2, 4, 2, 8, 2, CZ).transpose(0, 2, 4, 1, 3, 5, 6).reshape(2, 32, 128)
     vm = pl.BlockSpec(memory_space=pltpu.VMEM)
     sm = pl.BlockSpec(memory_space=pltpu.SMEM)
     hbm = pl.BlockSpec(memory_space=pl.ANY)
     dma = pltpu.SemaphoreType.DMA
-    decoded, latent, new_mid = pl.pallas_call(
+    parts = pl.pallas_call(
         functools.partial(kernel, n_dec, n_row),
         out_shape=(
-            jax.ShapeDtypeStruct((2, 4, 8, 16, 256), BF16),
+            jax.ShapeDtypeStruct((4, 2, 4, 32, 256), BF16),
             jax.ShapeDtypeStruct((2, 4, 16, 128), BF16),
-            jax.ShapeDtypeStruct((2, 2, 8, 16, 256), BF16),
+            jax.ShapeDtypeStruct((2, 2, 4, 32, 256), BF16),
         ),
         in_specs=[hbm, vm, vm, vm, hbm, sm, sm, vm, vm, vm, vm, hbm, vm],
         out_specs=(vm, vm, vm),
         scratch_shapes=[
+            pltpu.VMEM((2, 32, 128), BF16),
             pltpu.VMEM((256, depth), BF16),
             pltpu.VMEM((27, 512, 256), BF16),
             pltpu.VMEM((2, 4, 16, 128), F32),
@@ -573,25 +736,29 @@
             pltpu.VMEM((4, 4, 5, 16, 512), BF16),
             pltpu.VMEM((8, 512), F32),
             pltpu.VMEM((n_row - 1, 8, 512), F32),
-            pltpu.VMEM((slots, 2, 8, 16, 256), BF16),
+            pltpu.VMEM((slots, 8, 16, 256), BF16),
+            pltpu.VMEM((slots, 8, 16, 256), BF16),
+            pltpu.VMEM((2, 8, 32, 256), BF16),
             pltpu.VMEM((2, 10, 32, 512), BF16),
             pltpu.VMEM((2, 4, 6, 5, 16, 512), BF16),
             pltpu.VMEM((4, 4, 64, 256), F32),
-            dma((3,)),
+            dma((4,)),
             dma((n_dec - 1,)),
             dma((n_dec - 1,)),
-            dma((n_dec - 1,)),
-            dma((n_dec - 1,)),
-            dma((4,)),
-            dma((4,)),
+            dma((n_dec - 1, 2)),
+            dma((n_dec - 1, 2)),
+            dma((4, 2)),
+            dma((4, 2)),
+            dma((5,)),
+            dma((5,)),
             dma((5,)),
             dma((5,)),
             dma((2,)),
             dma((2,)),
             dma((n_row - 1,)),
             dma((n_row - 1,)),
-            dma((5,)),
-            dma((5,)),
+            dma((2, 5)),
+            dma((2, 5)),
         ],
         compiler_params=pltpu.CompilerParams(
             collective_id=0, has_side_effects=True, vmem_limit_bytes=56 * 1024 * 1024
@@ -601,9 +768,9 @@
         ),
     )(
         hidden.reshape(256, depth),
-        head_t,
-        bias,
-        lat,
+        head_weight.T,
+        head_bias.reshape(1, 64),
+        lat_cache,
         mid_cache,
         moves,
         span_index,
@@ -614,9 +781,18 @@
         mid_weight.reshape(27, 512, 256),
         mid_bias.reshape(1, 256),
     )
-    kept = latent[..., 64:].reshape(2, 4, 2, 8, 2, 2, CZ)
-    kept = kept.transpose(2, 0, 1, 4, 3, 5, 6).reshape(2, 2, 8, 16, CZ)
-    return decoded, kept, new_mid
+    return pl.pallas_call(
+        weave_kernel,
+        out_shape=(
+            jax.ShapeDtypeStruct((2, 4, 8, 16, 256), BF16),
+            jax.ShapeDtypeStruct((2, 2, 8, 16, CZ), BF16),
+            jax.ShapeDtypeStruct((2, 2, 8, 16, 256), BF16),
+        ),
+        in_specs=[vm, vm, vm],
+        out_specs=(vm, vm, vm),
+        compiler_params=pltpu.CompilerParams(vmem_limit_bytes=16 * 1024 * 1024),
+        cost_estimate=pl.CostEstimate(flops=30_000_000, bytes_accessed=1_600_000, transcendentals=0),
+    )(*parts)
 
 
 def solution(mesh):

time: 58.3 us -> 43.7 us (0.75)
  the two profiles are of different devices: /device:TPU:1 before, /device:TPU:0 now
where the time goes in v2:
time: 43.7 us; the launch traced here: 43.4 us
  Pallas kernels  40 us (92%)
  local copies, waits for them, and re-layouts  2.74 us (6%)
  between operations  0.65 us (1%)
    pallas_call x1, Pallas kernels, shards(): pl.pallas_call(functools.partial(kernel, n_dec, n_row), out_shape=(jax.Sh...  38.7 us
    unnamed x6, local copies, waits for them, and re-layouts  2.74 us
    pallas_call x1, Pallas kernels, shards(): pl.pallas_call(weave_kernel, out_shape=(jax.ShapeDtypeStruct((2, 4, 8, 16...  1.27 us

profile of v2, /device:TPU:0, one launch (start us, length us, event | category | flops | bytes accessed | tf_op | source)
XLA Modules:
  0.0 43.4 jit_solution(5082253617334346860)
XLA Ops:
  0.6 38.7 %shard_map.148 = (bf16[4,2,4,32,256]{4,3,2,1,0:T(8,128)(2,1)}, bf16[2,4,16,128]{3,2,1,0:T(8,128)(2,1)}, bf16[2,2,4,32,256]{4,3,2,1,0:T(8,128)(2,1)}) custom-call(bf16[256,2560]{1,0:T(8,128)(2,1)} %bitcast.10, bf16[64,2560]{1,0:T(8,128)(2,1)} %bitcast.11, f32[1,64]{1,0:T(1,128)} %bitcast.17, bf16[2,2,8,16,16]{4,3,2,1,0:T(8,128)(2,1)} %lat.1, ...), custom_call_target="tpu_custom_call" | custom-call | flops 8999999488 | bytes 12000000 | tf_op jit(solution)/shard_map/pallas_call | solution.py:713
  39.4 0.0 copy-start
  39.4 1.0 %copy-done = bf16[4,2,4,32,256]{4,3,2,1,0:T(8,128)(2,1)S(1)} copy-done((bf16[4,2,4,32,256]{4,3,2,1,0:T(8,128)(2,1)S(1)}, bf16[4,2,4,32,256]{4,3,2,1,0:T(8,128)(2,1)}, u32[]{:S(2)}) %copy-start) | copy-done | bytes 524312
  40.4 0.0 copy-start.1
  40.4 0.9 %copy-done.1 = bf16[2,2,4,32,256]{4,3,2,1,0:T(8,128)(2,1)S(1)} copy-done((bf16[2,2,4,32,256]{4,3,2,1,0:T(8,128)(2,1)S(1)}, bf16[2,2,4,32,256]{4,3,2,1,0:T(8,128)(2,1)}, u32[]{:S(2)}) %copy-start.1) | copy-done | bytes 262168
  41.4 0.0 copy-start.2
  41.4 0.8 %copy-done.2 = bf16[2,4,16,128]{3,2,1,0:T(8,128)(2,1)S(1)} copy-done((bf16[2,4,16,128]{3,2,1,0:T(8,128)(2,1)S(1)}, bf16[2,4,16,128]{3,2,1,0:T(8,128)(2,1)}, u32[]{:S(2)}) %copy-start.2) | copy-done | bytes 32792
  42.1 1.3 %shard_map.149 = (bf16[2,4,8,16,256]{4,3,2,1,0:T(8,128)(2,1)}, bf16[2,2,8,16,16]{4,3,2,1,0:T(8,128)(2,1)}, bf16[2,2,8,16,256]{4,3,2,1,0:T(8,128)(2,1)}) custom-call(bf16[4,2,4,32,256]{4,3,2,1,0:T(8,128)(2,1)S(1)} %copy-done, bf16[2,4,16,128]{3,2,1,0:T(8,128)(2,1)S(1)} %copy-done.2, bf16[2,2,4,32,256]{4,3,2,1,0:T(8,128)(2,1)S(1)} %copy-done.1), custom_call_target="tpu_custom_call" | custom-call | flops 30000000 | bytes 1600000 | tf_op jit(solution)/shard_map/pallas_call | solution.py:784
Async XLA Ops:
  39.4 1.0 %copy-start = (bf16[4,2,4,32,256]{4,3,2,1,0:T(8,128)(2,1)S(1)}, bf16[4,2,4,32,256]{4,3,2,1,0:T(8,128)(2,1)}, u32[]{:S(2)}) copy-start(bf16[4,2,4,32,256]{4,3,2,1,0:T(8,128)(2,1)} %get-tuple-element.6.decoded) | copy-start | bytes 1572868
  40.4 0.9 %copy-start.1 = (bf16[2,2,4,32,256]{4,3,2,1,0:T(8,128)(2,1)S(1)}, bf16[2,2,4,32,256]{4,3,2,1,0:T(8,128)(2,1)}, u32[]{:S(2)}) copy-start(bf16[2,2,4,32,256]{4,3,2,1,0:T(8,128)(2,1)} %get-tuple-element.8.new_mid) | copy-start | bytes 786436
  41.4 0.8 %copy-start.2 = (bf16[2,4,16,128]{3,2,1,0:T(8,128)(2,1)S(1)}, bf16[2,4,16,128]{3,2,1,0:T(8,128)(2,1)}, u32[]{:S(2)}) copy-start(bf16[2,4,16,128]{3,2,1,0:T(8,128)(2,1)} %get-tuple-element.7.new_lat) | copy-start | bytes 98308

commit v3 on v2

--- a/solution.py
+++ b/solution.py
@@ -41,6 +41,9 @@
     decoded,
     new_lat,
     new_mid,
+    dec_v,
+    nl_v,
+    nm_v,
     lat_pk,
     hid_v,
     midw_v,
@@ -50,7 +53,7 @@
     lat_all,
     lat_own,
     lat_h,
-    cw_all,
+    cw_in,
     par_all,
     wide,
     z,
@@ -112,7 +115,6 @@
     for c in own_mid:
         c.start()
     load_w = pltpu.make_async_copy(midw, midw_v, local_sem.at[3])
-    load_w.start()
 
     ri = lax.broadcasted_iota(jnp.int32, (CZ, 128), 0)
     ci = lax.broadcasted_iota(jnp.int32, (CZ, 128), 1)
@@ -140,6 +142,27 @@
         jnp.where(ci // 16 % 2 == 0, halves[0], halves[1]).astype(BF16).reshape(2, 32, 128)
     )
 
+    zero_slab = jnp.zeros((CZ, 256), BF16)
+
+    def build(source, target):
+        def one(a, carry):
+            for pp in range(2):
+                for qq in range(2):
+                    for pos in range(16):
+                        di, dj, p, q = pos // 8, pos // 4 % 2, pos // 2 % 2, pos % 2
+                        b = 2 * di + p - 1 + pp
+                        e = 2 * dj + q - 1 + qq
+                        if 0 <= b < 3 and 0 <= e < 3:
+                            slab = source[a * 9 + b * 3 + e]
+                        else:
+                            slab = zero_slab
+                        wide[pp * 2 + qq, a, pl.ds(pos * 16, 16), target] = slab
+            return carry
+
+        lax.fori_loop(0, 3, one, 0)
+
+    build(cw, lanes)
+
     pl.semaphore_wait(barrier, 1 + (n_dec - 1) + 2 * (n_row - 1))
 
     def remote(src, dst, ssem, rsem, dev):
@@ -196,14 +219,12 @@
 
     half = lax.rem(r, 2)
     half_lanes = pl.ds(pl.multiple_of(half * 128, 128), 128)
-    out_lanes = pl.ds(pl.multiple_of(s * 256 + half * 128, 128), 128)
-    in_lanes = pl.ds(pl.multiple_of(o * 256 + half * 128, 128), 128)
     cw_copy = remote(
-        cw.at[:, :, half_lanes], cw_all.at[:, :, out_lanes], w_s.at[0], w_r.at[0], (o, d, r)
+        cw.at[:, :, half_lanes], cw_in.at[:, :, half_lanes], w_s.at[0], w_r.at[0], (o, d, r)
     )
     cw_copy.start()
     cw_pass = remote(
-        cw_all.at[:, :, in_lanes], cw_all.at[:, :, in_lanes], w_s.at[4], w_r.at[4],
+        cw_in.at[:, :, half_lanes], cw_in.at[:, :, half_lanes], w_s.at[4], w_r.at[4],
         (s, d, r + 1 - 2 * half),
     )
     par_copies = [
@@ -216,20 +237,21 @@
 
         @pl.when(inner)
         def _():
-            for f in range(2):
+            for f in (1, 0):
                 cross_copy(f).start()
 
         @pl.when(jnp.logical_not(inner))
         def _():
-            for f in range(2):
+            for f in (1, 0):
                 end_copy(f).start()
 
     else:
         for k in range(1, n_dec):
-            for f in range(2):
+            for f in (1, 0):
                 mid_copy(k, d, f).start()
 
     load_hidden.wait()
+    load_w.start()
     head = lax.dot_general(
         hid_v[...],
         jnp.concatenate([head_t[...], jnp.zeros_like(head_t)], axis=0),
@@ -270,7 +292,6 @@
     full.start()
 
     lat_all[pl.ds(2 * d, 2)] = lat_pk[...]
-    cw_all[:, :, lanes] = cw[...]
     for n, ref in enumerate((cb, gain, gbias)):
         par_all[n, :, lanes] = ref[...]
 
@@ -296,27 +317,8 @@
     for n, ref in enumerate((cb, gain, gbias)):
         remote(ref, par_all.at[n, :, olanes], w_s.at[n + 1], w_r.at[n + 1], (o, d, r)).wait_recv()
     cw_pass.wait_recv()
-    zero_slab = jnp.zeros((CZ, 512), BF16)
-
-    def build(a, carry):
-        for pp in range(2):
-            for qq in range(2):
-                for di in range(2):
-                    for dj in range(2):
-                        for p in range(2):
-                            for q in range(2):
-                                b = 2 * di + p - 1 + pp
-                                e = 2 * dj + q - 1 + qq
-                                row = di * 128 + dj * 64 + p * 32 + q * 16
-                                if 0 <= b < 3 and 0 <= e < 3:
-                                    slab = cw_all[a * 9 + b * 3 + e]
-                                else:
-                                    slab = zero_slab
-                                wide[pp * 2 + qq, a, pl.ds(row, 16), :] = slab
-        return carry
-
-    lax.fori_loop(0, 3, build, 0)
-    pass_on(0)
+    build(cw_in, olanes)
+    pass_on(1)
 
     full.wait_recv()
 
@@ -368,7 +370,7 @@
 
     for t in range(2):
         own = part[t] + part_x[t] + bias
-        new_lat[t] = own.astype(BF16)
+        nl_v[t] = own.astype(BF16)
         place(1, 2 + t, 2, own)
         place(0, 2 + t, 2, ((part_h[0, 0, t] + part_h[0, 1, t] + bias) * up_live)[None])
         place(5, 2 + t, 2, ((part_h[1, 0, t] + part_h[1, 1, t] + bias) * down_live)[None])
@@ -376,20 +378,33 @@
     place(0, 0, 1, lat_h[0][None])
     place(5, 0, 1, lat_h[1][None])
 
+    out_lat = pltpu.make_async_copy(nl_v, new_lat, local_sem.at[4])
+    out_lat.start()
+
+    conv_bias = par_all[0]
+
+    def input_conv(pp, qq, row, count):
+        out = jnp.zeros((64 * count, 512), F32)
+        for a in range(3):
+            lhs = jnp.concatenate(
+                [
+                    z[qq, a : a + 4, row + di : row + di + count].reshape(64 * count, 128)
+                    for di in range(2)
+                ],
+                axis=1,
+            )
+            out = out + jnp.dot(lhs, wide[pp * 2 + qq, a], preferred_element_type=F32)
+        first = (out + conv_bias).astype(BF16)
+        h1[pp * 2 + qq, :, row : row + count] = first.reshape(4, count, 16, 512)
+        return first
+
     total = jnp.zeros((16, 512), F32)
     square = jnp.zeros((16, 512), F32)
-    conv_bias = par_all[0]
     for pp in range(2):
+        if pp == 1:
+            pass_on(0)
         for qq in range(2):
-            out = jnp.zeros((320, 512), F32)
-            for a in range(3):
-                lhs = jnp.concatenate(
-                    [z[qq, a : a + 4, di : di + 5].reshape(320, 128) for di in range(2)], axis=1
-                )
-                out = out + jnp.dot(lhs, wide[pp * 2 + qq, a], preferred_element_type=F32)
-            first = (out + conv_bias).astype(BF16)
-            h1[pp * 2 + qq] = first.reshape(4, 5, 16, 512)
-            mine = first.astype(F32).reshape(4, 5, 16, 512)[:, pp : pp + 4].reshape(16, 16, 512)
+            mine = input_conv(pp, qq, pp, 4).astype(F32).reshape(16, 16, 512)
             total = total + jnp.sum(mine, axis=0)
             square = square + jnp.sum(mine * mine, axis=0)
     stats[...] = jnp.concatenate(
@@ -408,7 +423,80 @@
     ]
     for c in stat_copies:
         c.start()
-    pass_on(1)
+    for pp in range(2):
+        for qq in range(2):
+            input_conv(pp, qq, 0 if pp == 1 else 4, 1)
+
+    zero_row = jnp.zeros((2, 32, 512), BF16)
+
+    @pl.when(jnp.logical_not(has_up))
+    def _():
+        pm[:, 0] = zero_row
+
+    @pl.when(jnp.logical_not(has_down))
+    def _():
+        pm[:, 9] = zero_row
+
+    def pm_full(f):
+        block = pm.at[f, 1:9, :, lanes]
+        return remote(block, block, pm_s.at[f, 0], pm_r.at[f, 0], (o, d, r))
+
+    def pm_up(f):
+        return [
+            remote(pm.at[f, 1, :, lanes], pm.at[f, 9, :, lanes], pm_s.at[f, 1 + n], pm_r.at[f, 1 + n], (dev, d, r - 1))
+            for n, dev in enumerate((s, o))
+        ]
+
+    def pm_down(f):
+        return [
+            remote(pm.at[f, 8, :, lanes], pm.at[f, 0, :, lanes], pm_s.at[f, 3 + n], pm_r.at[f, 3 + n], (dev, d, r + 1))
+            for n, dev in enumerate((s, o))
+        ]
+
+    def share(f, pick):
+        for st in range(2):
+            live = (span[st] > 0).astype(BF16)
+            pm[f, 1:9, pl.ds(16 * st, 16), lanes] = pick(st) * live
+        pm_full(f).start()
+
+        @pl.when(has_up)
+        def _():
+            for c in pm_up(f):
+                c.start()
+
+        @pl.when(has_down)
+        def _():
+            for c in pm_down(f):
+                c.start()
+
+    def share_inner(f):
+        if line:
+
+            @pl.when(inner)
+            def _():
+                own_mid[f].wait()
+                cross_copy(f).wait_recv()
+                pass_copy(f).wait_recv()
+                for st in range(2):
+                    sel[f, :, pl.ds(16 * st, 16), :] = gm[f][moves[2 * end + st]]
+                pick_copy(f, end).start()
+                share(f, lambda st: gm[f][moves[2 * d + st]])
+
+    def share_end(f):
+        if line:
+
+            @pl.when(jnp.logical_not(inner))
+            def _():
+                pick_copy(f, near).wait_recv()
+                share(f, lambda st: sel[f, :, pl.ds(16 * st, 16), :])
+
+        else:
+            own_mid[f].wait()
+            for k in range(1, n_dec):
+                mid_copy(k, lax.rem(d + n_dec - k, n_dec), f).wait_recv()
+            share(f, lambda st: gm[f][moves[2 * d + st]])
+
+    share_inner(1)
     for c in stat_copies:
         c.wait_recv()
     sums = stats[...]
@@ -451,110 +539,45 @@
 
     acc[...] = jnp.zeros_like(acc)
 
-    def conv(k, pairs):
-        b = k // 3
-        e = k % 3
+    def conv(b, pairs):
         for a, t0, nt in pairs:
             pieces = []
             for pp in range(2):
                 src = (b + 1) % 2 if pp == 0 else b % 2
                 off = b // 2 if pp == 0 else (b + 1) // 2
                 for qq in range(2):
-                    var = (e + 2) % 3 if qq == 0 else e + e // 2
+                    taps = (2, 0, 1) if qq == 0 else (0, 1, 3)
                     pieces.append(
-                        mb[src, var, t0 + a : t0 + a + nt, pl.ds(off, 4)].reshape(nt * 64, 512)
+                        jnp.concatenate(
+                            [
+                                mb[src, var, t0 + a : t0 + a + nt, pl.ds(off, 4)].reshape(nt * 64, 512)
+                                for var in taps
+                            ],
+                            axis=1,
+                        )
                     )
             lhs = jnp.concatenate(pieces, axis=0)
-            got = jnp.dot(lhs, midw_v[a * 9 + k], preferred_element_type=F32)
+            got = jnp.dot(lhs, midw_v[a * 3 + b], preferred_element_type=F32)
             acc[:, t0 : t0 + nt] += got.reshape(4, nt, 64, 256)
 
+    share_inner(0)
     load_w.wait()
 
-    def tap_late(k, carry):
-        conv(k, ((2, 0, 4),))
+    def tap_late(b, carry):
+        conv(b, ((2, 0, 4),))
         return carry
 
-    zero_row = jnp.zeros((2, 32, 512), BF16)
-
-    @pl.when(jnp.logical_not(has_up))
-    def _():
-        pm[:, 0] = zero_row
-
-    @pl.when(jnp.logical_not(has_down))
-    def _():
-        pm[:, 9] = zero_row
-
-    def pm_full(f):
-        block = pm.at[f, 1:9, :, lanes]
-        return remote(block, block, pm_s.at[f, 0], pm_r.at[f, 0], (o, d, r))
-
-    def pm_up(f):
-        return [
-            remote(pm.at[f, 1, :, lanes], pm.at[f, 9, :, lanes], pm_s.at[f, 1 + n], pm_r.at[f, 1 + n], (dev, d, r - 1))
-            for n, dev in enumerate((s, o))
-        ]
-
-    def pm_down(f):
-        return [
-            remote(pm.at[f, 8, :, lanes], pm.at[f, 0, :, lanes], pm_s.at[f, 3 + n], pm_r.at[f, 3 + n], (dev, d, r + 1))
-            for n, dev in enumerate((s, o))
-        ]
-
-    def share(f, pick):
-        for st in range(2):
-            live = (span[st] > 0).astype(BF16)
-            pm[f, 1:9, pl.ds(16 * st, 16), lanes] = pick(st) * live
-        pm_full(f).start()
-
-        @pl.when(has_up)
-        def _():
-            for c in pm_up(f):
-                c.start()
-
-        @pl.when(has_down)
-        def _():
-            for c in pm_down(f):
-                c.start()
-
-    def share_inner(f):
-        if line:
-
-            @pl.when(inner)
-            def _():
-                own_mid[f].wait()
-                cross_copy(f).wait_recv()
-                pass_copy(f).wait_recv()
-                for st in range(2):
-                    sel[f, :, pl.ds(16 * st, 16), :] = gm[f][moves[2 * end + st]]
-                pick_copy(f, end).start()
-                share(f, lambda st: gm[f][moves[2 * d + st]])
-
-    def share_end(f):
-        if line:
-
-            @pl.when(jnp.logical_not(inner))
-            def _():
-                pick_copy(f, near).wait_recv()
-                share(f, lambda st: sel[f, :, pl.ds(16 * st, 16), :])
-
-        else:
-            own_mid[f].wait()
-            for k in range(1, n_dec):
-                mid_copy(k, lax.rem(d + n_dec - k, n_dec), f).wait_recv()
-            share(f, lambda st: gm[f][moves[2 * d + st]])
-
-    share_inner(0)
-    lax.fori_loop(0, 4, tap_late, 0)
-    share_inner(1)
-    lax.fori_loop(4, 9, tap_late, 0)
+    lax.fori_loop(0, 1, tap_late, 0)
+    share_end(1)
+    lax.fori_loop(1, 2, tap_late, 0)
     share_end(0)
-    share_end(1)
+    lax.fori_loop(2, 3, tap_late, 0)
 
     def tap_mid(k, carry):
         conv(k, ((1, 1, 3), (0, 2, 2)))
         return carry
 
-    lax.fori_loop(0, 9, tap_mid, 0)
+    lax.fori_loop(0, 3, tap_mid, 0)
 
     ro = lax.broadcasted_iota(jnp.int32, (64, 32), 0)
     co = lax.broadcasted_iota(jnp.int32, (64, 32), 1)
@@ -567,35 +590,9 @@
     for t in range(2):
         for pp in range(2):
             for qq in range(2):
-                new_mid[t, pp, :, pl.ds(16 * qq, 16), :] = mb[pp, qq, t + 4, pp : pp + 4, :, lanes]
-
-    for f in range(2):
-        pm_full(f).wait_recv()
-
-        @pl.when(has_up)
-        def _():
-            for c in pm_down(f):
-                c.wait_recv()
-
-        @pl.when(has_down)
-        def _():
-            for c in pm_up(f):
-                c.wait_recv()
-
-    def unfold(f, carry):
-        for row in range(10):
-            y = jnp.dot(deal, pm[f, row], preferred_element_type=F32).astype(BF16)
-            for v in range(4):
-                mb[(row + 1) % 2, v, f, row // 2] = y[16 * v : 16 * v + 16]
-        return carry
-
-    lax.fori_loop(0, 2, unfold, 0)
-
-    def tap_early(k, carry):
-        conv(k, ((1, 0, 1), (0, 0, 2)))
-        return carry
-
-    lax.fori_loop(0, 9, tap_early, 0)
+                nm_v[t, pp, :, pl.ds(16 * qq, 16), :] = mb[pp, qq, t + 4, pp : pp + 4, :, lanes]
+    out_mid = pltpu.make_async_copy(nm_v, new_mid, local_sem.at[5])
+    out_mid.start()
 
     def finish(t, carry):
         for pp in range(2):
@@ -605,10 +602,44 @@
                     + acc[pp * 2 + qq, t].reshape(4, 16, 256)
                     + midb[...]
                 )
-                decoded[t, pp, :, pl.ds(16 * qq, 16), :] = y.astype(BF16)
+                dec_v[t, pp, :, pl.ds(16 * qq, 16), :] = y.astype(BF16)
         return carry
 
-    lax.fori_loop(0, 4, finish, 0)
+    lax.fori_loop(2, 4, finish, 0)
+    out_late = pltpu.make_async_copy(
+        dec_v.at[pl.ds(2, 2)], decoded.at[pl.ds(2, 2)], local_sem.at[6]
+    )
+    out_late.start()
+
+    for f, pairs in ((1, ((1, 0, 1), (0, 1, 1))), (0, ((0, 0, 1),))):
+        pm_full(f).wait_recv()
+
+        @pl.when(has_up)
+        def _():
+            for c in pm_down(f):
+                c.wait_recv()
+
+        @pl.when(has_down)
+        def _():
+            for c in pm_up(f):
+                c.wait_recv()
+
+        for row in range(10):
+            y = jnp.dot(deal, pm[f, row], preferred_element_type=F32).astype(BF16)
+            for v in range(4):
+                mb[(row + 1) % 2, v, f, row // 2] = y[16 * v : 16 * v + 16]
+
+        def tap_early(b, carry):
+            conv(b, pairs)
+            return carry
+
+        lax.fori_loop(0, 3, tap_early, 0)
+
+    lax.fori_loop(0, 2, finish, 0)
+    out_early = pltpu.make_async_copy(
+        dec_v.at[pl.ds(0, 2)], decoded.at[pl.ds(0, 2)], local_sem.at[7]
+    )
+    out_early.start()
 
     for k in range(1, n_dec):
         lat_copy(k, d).wait_send()
@@ -643,9 +674,21 @@
     def _():
         for c in down + pm_down(0) + pm_down(1) + [lat_edge_down]:
             c.wait_send()
-
-
-def weave_kernel(decoded, new_lat, new_mid, decoded_out, new_lat_out, new_mid_out):
+    for c in (out_lat, out_mid, out_late, out_early):
+        c.wait()
+
+
+def weave_kernel(
+    decoded_in, new_lat_in, new_mid_in, decoded_out, new_lat_out, new_mid_out, decoded, new_lat, new_mid, sem
+):
+    loads = [
+        pltpu.make_async_copy(source, target, sem.at[n])
+        for n, (source, target) in enumerate(
+            ((new_lat_in, new_lat), (new_mid_in, new_mid), (decoded_in, decoded))
+        )
+    ]
+    for c in loads:
+        c.start()
     ro = lax.broadcasted_iota(jnp.int32, (32, 32), 0)
     co = lax.broadcasted_iota(jnp.int32, (32, 32), 1)
     weave = jnp.where(co == (ro % 2) * 16 + (ro // 16) * 8 + (ro % 16) // 2, 1.0, 0.0).astype(BF16)
@@ -657,11 +700,7 @@
                 target[0, t, 2 * i + pp] = y[0:16]
                 target[1, t, 2 * i + pp] = y[16:32]
 
-    for t in range(4):
-        spread(decoded, decoded_out, t)
-    for t in range(2):
-        spread(new_mid, new_mid_out, t)
-
+    loads[0].wait()
     patches = new_lat[...].reshape(128, 128)
     ro = lax.broadcasted_iota(jnp.int32, (256, 128), 0)
     co = lax.broadcasted_iota(jnp.int32, (256, 128), 1)
@@ -685,6 +724,12 @@
                 for st in range(2):
                     row = ((t * 4 + i) * 2 + st) * 16
                     new_lat_out[st, t, 2 * i + p] = y[row : row + 16]
+    loads[1].wait()
+    for t in range(2):
+        spread(new_mid, new_mid_out, t)
+    loads[2].wait()
+    for t in range(4):
+        spread(decoded, decoded_out, t)
 
 
 def shards(
@@ -718,18 +763,21 @@
             jax.ShapeDtypeStruct((2, 2, 4, 32, 256), BF16),
         ),
         in_specs=[hbm, vm, vm, vm, hbm, sm, sm, vm, vm, vm, vm, hbm, vm],
-        out_specs=(vm, vm, vm),
+        out_specs=(hbm, hbm, hbm),
         scratch_shapes=[
+            pltpu.VMEM((4, 2, 4, 32, 256), BF16),
+            pltpu.VMEM((2, 4, 16, 128), BF16),
+            pltpu.VMEM((2, 2, 4, 32, 256), BF16),
             pltpu.VMEM((2, 32, 128), BF16),
             pltpu.VMEM((256, depth), BF16),
-            pltpu.VMEM((27, 512, 256), BF16),
+            pltpu.VMEM((9, 1536, 256), BF16),
             pltpu.VMEM((2, 4, 16, 128), F32),
             pltpu.VMEM((2, 4, 16, 128), F32),
             pltpu.VMEM((2, 2, 2, 16, 128), F32),
             pltpu.VMEM((slots, 32, 128), BF16),
             pltpu.VMEM((4, 16, 128), F32),
             pltpu.VMEM((2, 16, 128), F32),
-            pltpu.VMEM((27, CZ, 512), BF16),
+            pltpu.VMEM((27, CZ, 256), BF16),
             pltpu.VMEM((3, 1, 512), F32),
             pltpu.VMEM((4, 3, 256, 512), BF16),
             pltpu.VMEM((2, 6, 6, 16, 128), BF16),
@@ -742,7 +790,7 @@
             pltpu.VMEM((2, 10, 32, 512), BF16),
             pltpu.VMEM((2, 4, 6, 5, 16, 512), BF16),
             pltpu.VMEM((4, 4, 64, 256), F32),
-            dma((4,)),
+            dma((8,)),
             dma((n_dec - 1,)),
             dma((n_dec - 1,)),
             dma((n_dec - 1, 2)),
@@ -778,7 +826,7 @@
         conv_in_bias.reshape(1, 256),
         gn_gain.reshape(1, 256),
         gn_bias.reshape(1, 256),
-        mid_weight.reshape(27, 512, 256),
+        mid_weight.reshape(9, 1536, 256),
         mid_bias.reshape(1, 256),
     )
     return pl.pallas_call(
@@ -788,9 +836,15 @@
             jax.ShapeDtypeStruct((2, 2, 8, 16, CZ), BF16),
             jax.ShapeDtypeStruct((2, 2, 8, 16, 256), BF16),
         ),
-        in_specs=[vm, vm, vm],
+        in_specs=[hbm, hbm, hbm],
         out_specs=(vm, vm, vm),
-        compiler_params=pltpu.CompilerParams(vmem_limit_bytes=16 * 1024 * 1024),
+        scratch_shapes=[
+            pltpu.VMEM((4, 2, 4, 32, 256), BF16),
+            pltpu.VMEM((2, 4, 16, 128), BF16),
+            pltpu.VMEM((2, 2, 4, 32, 256), BF16),
+            dma((3,)),
+        ],
+        compiler_params=pltpu.CompilerParams(vmem_limit_bytes=60 * 1024 * 1024),
         cost_estimate=pl.CostEstimate(flops=30_000_000, bytes_accessed=1_600_000, transcendentals=0),
     )(*parts)
 

time: 43.7 us -> 39.2 us (0.90)
  local copies, waits for them, and re-layouts: 2.74 us -> 0 us
  Pallas kernels: 40 us -> 38.4 us
    unnamed x6 -> x0, local copies, waits for them, and re-layouts: 2.74 us -> none
    pallas_call x1, Pallas kernels: 38.7 us -> 36 us  [shards(): pl.pallas_call(functools.partial(kernel, n_dec, n_row), out_shape=(jax.Sh...]
    pallas_call x1, Pallas kernels: 1.27 us -> 2.37 us  [shards(): pl.pallas_call(weave_kernel, out_shape=(jax.ShapeDtypeStruct((2, 4, 8, 16...]
where the time goes in v3:
time: 39.2 us; the launch traced here: 39 us
  Pallas kernels  38.4 us (98%)
  between operations  0.64 us (2%)
    pallas_call x1, Pallas kernels, shards(): pl.pallas_call(functools.partial(kernel, n_dec, n_row), out_shape=(jax.Sh...  36 us
    pallas_call x1, Pallas kernels, shards(): pl.pallas_call(weave_kernel, out_shape=(jax.ShapeDtypeStruct((2, 4, 8, 16...  2.37 us

profile of v3, /device:TPU:0, one launch (start us, length us, event | category | flops | bytes accessed | tf_op | source)
XLA Modules:
  0.0 39.0 jit_solution(13029600332105990192)
XLA Ops:
  0.6 36.0 %shard_map.148 = (bf16[4,2,4,32,256]{4,3,2,1,0:T(8,128)(2,1)}, bf16[2,4,16,128]{3,2,1,0:T(8,128)(2,1)}, bf16[2,2,4,32,256]{4,3,2,1,0:T(8,128)(2,1)}) custom-call(bf16[256,2560]{1,0:T(8,128)(2,1)} %bitcast.10, bf16[64,2560]{1,0:T(8,128)(2,1)} %bitcast.11, f32[1,64]{1,0:T(1,128)} %bitcast.17, bf16[2,2,8,16,16]{4,3,2,1,0:T(8,128)(2,1)} %lat.1, ...), custom_call_target="tpu_custom_call" | custom-call | flops 8999999488 | bytes 12000000 | tf_op jit(solution)/shard_map/pallas_call | solution.py:758
  36.6 2.4 %shard_map.149 = (bf16[2,4,8,16,256]{4,3,2,1,0:T(8,128)(2,1)}, bf16[2,2,8,16,16]{4,3,2,1,0:T(8,128)(2,1)}, bf16[2,2,8,16,256]{4,3,2,1,0:T(8,128)(2,1)}) custom-call(bf16[4,2,4,32,256]{4,3,2,1,0:T(8,128)(2,1)} %get-tuple-element.6.decoded_in, bf16[2,4,16,128]{3,2,1,0:T(8,128)(2,1)} %get-tuple-element.7.new_lat_in, ...), custom_call_target="tpu_custom_call" | custom-call | flops 30000000 | bytes 1600000 | tf_op jit(solution)/shard_map/pallas_call | solution.py:832

commit v4 on v3

--- a/solution.py
+++ b/solution.py
@@ -116,6 +116,73 @@
         c.start()
     load_w = pltpu.make_async_copy(midw, midw_v, local_sem.at[3])
 
+    pl.semaphore_wait(barrier, 1 + (n_dec - 1) + 2 * (n_row - 1))
+
+    def remote(src, dst, ssem, rsem, dev):
+        return pltpu.make_async_remote_copy(
+            src_ref=src, dst_ref=dst, send_sem=ssem, recv_sem=rsem, device_id=dev, device_id_type=MESH
+        )
+
+    def lat_copy(k, origin):
+        return remote(
+            lat_pk, lat_all.at[pl.ds(2 * origin, 2)], lat_s.at[k - 1], lat_r.at[k - 1],
+            (s, lax.rem(d + k, n_dec), r),
+        )
+
+    def mid_copy(k, origin, f):
+        return remote(
+            mid.at[:, f], gm[f].at[pl.ds(2 * origin, 2)], mid_s.at[k - 1, f], mid_r.at[k - 1, f],
+            (s, lax.rem(d + k, n_dec), r),
+        )
+
+    line = n_dec == 4
+    inner = (d == 1) | (d == 2)
+    end = 3 * (d - 1)
+    near = 1 + d // 3
+
+    def end_copy(f):
+        return remote(
+            mid.at[:, f], gm[f].at[pl.ds(2 * d, 2)], hop_s.at[0, f], hop_r.at[0, f], (s, near, r)
+        )
+
+    def cross_copy(f):
+        return remote(
+            mid.at[:, f], gm[f].at[pl.ds(2 * d, 2)], hop_s.at[1, f], hop_r.at[1, f], (s, 3 - d, r)
+        )
+
+    def pass_copy(f):
+        slots = pl.ds(2 * end, 2)
+        return remote(
+            gm[f].at[slots], gm[f].at[slots], hop_s.at[2, f], hop_r.at[2, f], (s, 3 - d, r)
+        )
+
+    def pick_copy(f, target):
+        return remote(sel.at[f], sel.at[f], hop_s.at[3, f], hop_r.at[3, f], (s, target, r))
+
+    def pass_on(f):
+        if line:
+
+            @pl.when(inner)
+            def _():
+                end_copy(f).wait_recv()
+                pass_copy(f).start()
+
+    half = lax.rem(r, 2)
+    half_lanes = pl.ds(pl.multiple_of(half * 128, 128), 128)
+    cw_copy = remote(
+        cw.at[:, :, half_lanes], cw_in.at[:, :, half_lanes], w_s.at[0], w_r.at[0], (o, d, r)
+    )
+    cw_copy.start()
+    cw_pass = remote(
+        cw_in.at[:, :, half_lanes], cw_in.at[:, :, half_lanes], w_s.at[4], w_r.at[4],
+        (s, d, r + 1 - 2 * half),
+    )
+    par_copies = [
+        remote(ref, par_all.at[n, :, lanes], w_s.at[n + 1], w_r.at[n + 1], (o, d, r))
+        for n, ref in enumerate((cb, gain, gbias))
+    ]
+    for c in par_copies:
+        c.start()
     ri = lax.broadcasted_iota(jnp.int32, (CZ, 128), 0)
     ci = lax.broadcasted_iota(jnp.int32, (CZ, 128), 1)
     tile = jnp.where(ci % CZ == ri, 1.0, 0.0).astype(BF16)
@@ -141,6 +208,67 @@
     lat_pk[...] = (
         jnp.where(ci // 16 % 2 == 0, halves[0], halves[1]).astype(BF16).reshape(2, 32, 128)
     )
+
+    for k in range(1, n_dec):
+        lat_copy(k, d).start()
+
+    if line:
+
+        @pl.when(inner)
+        def _():
+            for f in (1, 0):
+                cross_copy(f).start()
+
+        @pl.when(jnp.logical_not(inner))
+        def _():
+            for f in (1, 0):
+                end_copy(f).start()
+
+    else:
+        for k in range(1, n_dec):
+            for f in (1, 0):
+                mid_copy(k, d, f).start()
+
+    load_hidden.wait()
+    load_w.start()
+    head = lax.dot_general(
+        hid_v[...],
+        jnp.concatenate([head_t[...], jnp.zeros_like(head_t)], axis=0),
+        (((1,), (1,)), ((), ())),
+        preferred_element_type=F32,
+    )
+    head = head.reshape(2, 4, 4, 8, 128)
+    lane = lax.broadcasted_iota(jnp.int32, (4, 8, 128), 2)
+    for t in range(2):
+        for st in range(2):
+            high = pltpu.roll(head[st, t + 2].reshape(32, 128), 64, 1).reshape(4, 8, 128)
+            part[t, :, pl.ds(8 * st, 8), :] = jnp.where(lane < 64, head[st, t], high)
+
+    def part_copies():
+        full = remote(part, part_x, part_s.at[0], part_r.at[0], (o, d, r))
+        up = [
+            remote(part.at[:, 0], part_h.at[1, n], part_s.at[1 + n], part_r.at[1 + n], (dev, d, r - 1))
+            for n, dev in enumerate((s, o))
+        ]
+        down = [
+            remote(part.at[:, 3], part_h.at[0, n], part_s.at[3 + n], part_r.at[3 + n], (dev, d, r + 1))
+            for n, dev in enumerate((s, o))
+        ]
+        return full, up, down
+
+    full, up, down = part_copies()
+
+    @pl.when(has_up)
+    def _():
+        for c in up:
+            c.start()
+
+    @pl.when(has_down)
+    def _():
+        for c in down:
+            c.start()
+
+    full.start()
 
     zero_slab = jnp.zeros((CZ, 256), BF16)
 
@@ -162,135 +290,6 @@
         lax.fori_loop(0, 3, one, 0)
 
     build(cw, lanes)
-
-    pl.semaphore_wait(barrier, 1 + (n_dec - 1) + 2 * (n_row - 1))
-
-    def remote(src, dst, ssem, rsem, dev):
-        return pltpu.make_async_remote_copy(
-            src_ref=src, dst_ref=dst, send_sem=ssem, recv_sem=rsem, device_id=dev, device_id_type=MESH
-        )
-
-    def lat_copy(k, origin):
-        return remote(
-            lat_pk, lat_all.at[pl.ds(2 * origin, 2)], lat_s.at[k - 1], lat_r.at[k - 1],
-            (s, lax.rem(d + k, n_dec), r),
-        )
-
-    def mid_copy(k, origin, f):
-        return remote(
-            mid.at[:, f], gm[f].at[pl.ds(2 * origin, 2)], mid_s.at[k - 1, f], mid_r.at[k - 1, f],
-            (s, lax.rem(d + k, n_dec), r),
-        )
-
-    line = n_dec == 4
-    inner = (d == 1) | (d == 2)
-    end = 3 * (d - 1)
-    near = 1 + d // 3
-
-    def end_copy(f):
-        return remote(
-            mid.at[:, f], gm[f].at[pl.ds(2 * d, 2)], hop_s.at[0, f], hop_r.at[0, f], (s, near, r)
-        )
-
-    def cross_copy(f):
-        return remote(
-            mid.at[:, f], gm[f].at[pl.ds(2 * d, 2)], hop_s.at[1, f], hop_r.at[1, f], (s, 3 - d, r)
-        )
-
-    def pass_copy(f):
-        slots = pl.ds(2 * end, 2)
-        return remote(
-            gm[f].at[slots], gm[f].at[slots], hop_s.at[2, f], hop_r.at[2, f], (s, 3 - d, r)
-        )
-
-    def pick_copy(f, target):
-        return remote(sel.at[f], sel.at[f], hop_s.at[3, f], hop_r.at[3, f], (s, target, r))
-
-    def pass_on(f):
-        if line:
-
-            @pl.when(inner)
-            def _():
-                end_copy(f).wait_recv()
-                pass_copy(f).start()
-
-    for k in range(1, n_dec):
-        lat_copy(k, d).start()
-
-    half = lax.rem(r, 2)
-    half_lanes = pl.ds(pl.multiple_of(half * 128, 128), 128)
-    cw_copy = remote(
-        cw.at[:, :, half_lanes], cw_in.at[:, :, half_lanes], w_s.at[0], w_r.at[0], (o, d, r)
-    )
-    cw_copy.start()
-    cw_pass = remote(
-        cw_in.at[:, :, half_lanes], cw_in.at[:, :, half_lanes], w_s.at[4], w_r.at[4],
-        (s, d, r + 1 - 2 * half),
-    )
-    par_copies = [
-        remote(ref, par_all.at[n, :, lanes], w_s.at[n + 1], w_r.at[n + 1], (o, d, r))
-        for n, ref in enumerate((cb, gain, gbias))
-    ]
-    for c in par_copies:
-        c.start()
-    if line:
-
-        @pl.when(inner)
-        def _():
-            for f in (1, 0):
-                cross_copy(f).start()
-
-        @pl.when(jnp.logical_not(inner))
-        def _():
-            for f in (1, 0):
-                end_copy(f).start()
-
-    else:
-        for k in range(1, n_dec):
-            for f in (1, 0):
-                mid_copy(k, d, f).start()
-
-    load_hidden.wait()
-    load_w.start()
-    head = lax.dot_general(
-        hid_v[...],
-        jnp.concatenate([head_t[...], jnp.zeros_like(head_t)], axis=0),
-        (((1,), (1,)), ((), ())),
-        preferred_element_type=F32,
-    )
-    head = head.reshape(2, 4, 4, 8, 128)
-    lane = lax.broadcasted_iota(jnp.int32, (4, 8, 128), 2)
-    for t in range(2):
-        for st in range(2):
-            high = pltpu.roll(head[st, t + 2].reshape(32, 128), 64, 1).reshape(4, 8, 128)
-            part[t, :, pl.ds(8 * st, 8), :] = jnp.where(lane < 64, head[st, t], high)
-
-    def part_copies():
-        full = remote(part, part_x, part_s.at[0], part_r.at[0], (o, d, r))
-        up = [
-            remote(part.at[:, 0], part_h.at[1, n], part_s.at[1 + n], part_r.at[1 + n], (dev, d, r - 1))
-            for n, dev in enumerate((s, o))
-        ]
-        down = [
-            remote(part.at[:, 3], part_h.at[0, n], part_s.at[3 + n], part_r.at[3 + n], (dev, d, r + 1))
-            for n, dev in enumerate((s, o))
-        ]
-        return full, up, down
-
-    full, up, down = part_copies()
-
-    @pl.when(has_up)
-    def _():
-        for c in up:
-            c.start()
-
-    @pl.when(has_down)
-    def _():
-        for c in down:
-            c.start()
-
-    full.start()
-
     lat_all[pl.ds(2 * d, 2)] = lat_pk[...]
     for n, ref in enumerate((cb, gain, gbias)):
         par_all[n, :, lanes] = ref[...]
@@ -314,10 +313,6 @@
 
     cw_copy.wait_recv()
     cw_pass.start()
-    for n, ref in enumerate((cb, gain, gbias)):
-        remote(ref, par_all.at[n, :, olanes], w_s.at[n + 1], w_r.at[n + 1], (o, d, r)).wait_recv()
-    cw_pass.wait_recv()
-    build(cw_in, olanes)
     pass_on(1)
 
     full.wait_recv()
@@ -381,10 +376,8 @@
     out_lat = pltpu.make_async_copy(nl_v, new_lat, local_sem.at[4])
     out_lat.start()
 
-    conv_bias = par_all[0]
-
-    def input_conv(pp, qq, row, count):
-        out = jnp.zeros((64 * count, 512), F32)
+    def input_conv(pp, qq, row, count, part_lanes):
+        out = jnp.zeros((64 * count, 256), F32)
         for a in range(3):
             lhs = jnp.concatenate(
                 [
@@ -393,39 +386,51 @@
                 ],
                 axis=1,
             )
-            out = out + jnp.dot(lhs, wide[pp * 2 + qq, a], preferred_element_type=F32)
-        first = (out + conv_bias).astype(BF16)
-        h1[pp * 2 + qq, :, row : row + count] = first.reshape(4, count, 16, 512)
+            out = out + jnp.dot(lhs, wide[pp * 2 + qq, a, :, part_lanes], preferred_element_type=F32)
+        first = (out + par_all[0, :, part_lanes]).astype(BF16)
+        h1[pp * 2 + qq, :, row : row + count, :, part_lanes] = first.reshape(4, count, 16, 256)
         return first
 
-    total = jnp.zeros((16, 512), F32)
-    square = jnp.zeros((16, 512), F32)
-    for pp in range(2):
-        if pp == 1:
-            pass_on(0)
-        for qq in range(2):
-            mine = input_conv(pp, qq, pp, 4).astype(F32).reshape(16, 16, 512)
-            total = total + jnp.sum(mine, axis=0)
-            square = square + jnp.sum(mine * mine, axis=0)
-    stats[...] = jnp.concatenate(
-        [
-            jnp.sum(total[0:8], axis=0, keepdims=True),
-            jnp.sum(total[8:16], axis=0, keepdims=True),
-            jnp.sum(square[0:8], axis=0, keepdims=True),
-            jnp.sum(square[8:16], axis=0, keepdims=True),
-            jnp.zeros((4, 512), F32),
-        ],
-        axis=0,
-    )
-    stat_copies = [
-        remote(stats, stats_in.at[k - 1], st_s.at[k - 1], st_r.at[k - 1], (s, d, lax.rem(r + k, n_row)))
-        for k in range(1, n_row)
-    ]
-    for c in stat_copies:
-        c.start()
-    for pp in range(2):
-        for qq in range(2):
-            input_conv(pp, qq, 0 if pp == 1 else 4, 1)
+    def stat_copies(n):
+        return [
+            remote(
+                stats.at[n], stats_in.at[n, k - 1], st_s.at[n, k - 1], st_r.at[n, k - 1],
+                (s, d, lax.rem(r + k, n_row)),
+            )
+            for k in range(1, n_row)
+        ]
+
+    def input_half(n, part_lanes):
+        total = jnp.zeros((16, 256), F32)
+        square = jnp.zeros((16, 256), F32)
+        for pp in range(2):
+            for qq in range(2):
+                mine = input_conv(pp, qq, pp, 4, part_lanes).astype(F32).reshape(16, 16, 256)
+                total = total + jnp.sum(mine, axis=0)
+                square = square + jnp.sum(mine * mine, axis=0)
+        stats[n] = jnp.concatenate(
+            [
+                jnp.sum(total[0:8], axis=0, keepdims=True),
+                jnp.sum(total[8:16], axis=0, keepdims=True),
+                jnp.sum(square[0:8], axis=0, keepdims=True),
+                jnp.sum(square[8:16], axis=0, keepdims=True),
+                jnp.zeros((4, 256), F32),
+            ],
+            axis=0,
+        )
+        for c in stat_copies(n):
+            c.start()
+        for pp in range(2):
+            for qq in range(2):
+                input_conv(pp, qq, 0 if pp == 1 else 4, 1, part_lanes)
+
+    input_half(0, lanes)
+    pass_on(0)
+    cw_pass.wait_recv()
+    build(cw_in, olanes)
+    for n, ref in enumerate((cb, gain, gbias)):
+        remote(ref, par_all.at[n, :, olanes], w_s.at[n + 1], w_r.at[n + 1], (o, d, r)).wait_recv()
+    input_half(1, olanes)
 
     zero_row = jnp.zeros((2, 32, 512), BF16)
 
@@ -497,45 +502,52 @@
             share(f, lambda st: gm[f][moves[2 * d + st]])
 
     share_inner(1)
-    for c in stat_copies:
-        c.wait_recv()
-    sums = stats[...]
-    for k in range(1, n_row):
-        sums = sums + stats_in[k - 1]
-    lane8 = lax.broadcasted_iota(jnp.int32, (8, 512), 1)
-    for k in (1, 2, 4, 8):
-        other = jnp.where((lane8 & k) > 0, pltpu.roll(sums, k, 1), pltpu.roll(sums, 512 - k, 1))
-        sums = sums + other
-    sums = sums / (4 * 8 * 16 * GROUP * n_row)
-    gv = sums[2:4] - sums[0:2] * sums[0:2]
-    scale = lax.rsqrt(gv + 1e-5) * par_all[1]
-    shift = par_all[2]
-
-    def spread(v):
-        return jnp.concatenate(
-            [jnp.broadcast_to(v[0:1], (8, 512)), jnp.broadcast_to(v[1:2], (8, 512))], axis=0
-        )
-
-    mean16 = spread(sums[0:2])
-    scale16 = spread(scale)
-
-    def activate(t, carry):
-        for pp in range(2):
-            for qq in range(2):
-                v = (h1[pp * 2 + qq, t].astype(F32) - mean16) * scale16 + shift
-                v = v * (0.5 * jnp.tanh(0.5 * v) + 0.5)
-                edge = lax.broadcasted_iota(jnp.int32, (5, 16, 512), 0)
-                if pp == 1:
-                    v = jnp.where((edge == 0) & jnp.logical_not(has_up), 0.0, v)
-                else:
-                    v = jnp.where((edge == 4) & jnp.logical_not(has_down), 0.0, v)
-                v = v.astype(BF16)
-                mb[pp, qq, t + 2] = v
-                moved = shifted(v.astype(F32).reshape(80, 512), -1 if qq == 1 else 1)
-                mb[pp, 2 if qq == 1 else 3, t + 2] = moved.astype(BF16).reshape(5, 16, 512)
-        return carry
-
-    lax.fori_loop(0, 4, activate, 0)
+
+    def activate_half(n, part_lanes):
+        for c in stat_copies(n):
+            c.wait_recv()
+        sums = stats[n]
+        for k in range(1, n_row):
+            sums = sums + stats_in[n, k - 1]
+        lane8 = lax.broadcasted_iota(jnp.int32, (8, 256), 1)
+        for k in (1, 2, 4, 8):
+            other = jnp.where((lane8 & k) > 0, pltpu.roll(sums, k, 1), pltpu.roll(sums, 256 - k, 1))
+            sums = sums + other
+        sums = sums / (4 * 8 * 16 * GROUP * n_row)
+        gv = sums[2:4] - sums[0:2] * sums[0:2]
+        scale = lax.rsqrt(gv + 1e-5) * par_all[1, :, part_lanes]
+        shift = par_all[2, :, part_lanes]
+
+        def spread(v):
+            return jnp.concatenate(
+                [jnp.broadcast_to(v[0:1], (8, 256)), jnp.broadcast_to(v[1:2], (8, 256))], axis=0
+            )
+
+        mean16 = spread(sums[0:2])
+        scale16 = spread(scale)
+
+        def activate(t, carry):
+            for pp in range(2):
+                for qq in range(2):
+                    v = (h1[pp * 2 + qq, t, :, :, part_lanes].astype(F32) - mean16) * scale16 + shift
+                    v = v * (0.5 * jnp.tanh(0.5 * v) + 0.5)
+                    edge = lax.broadcasted_iota(jnp.int32, (5, 16, 256), 0)
+                    if pp == 1:
+                        v = jnp.where((edge == 0) & jnp.logical_not(has_up), 0.0, v)
+                    else:
+                        v = jnp.where((edge == 4) & jnp.logical_not(has_down), 0.0, v)
+                    v = v.astype(BF16)
+                    mb[pp, qq, t + 2, :, :, part_lanes] = v
+                    moved = shifted(v.astype(F32).reshape(80, 256), -1 if qq == 1 else 1)
+                    mb[pp, 2 if qq == 1 else 3, t + 2, :, :, part_lanes] = moved.astype(BF16).reshape(
+                        5, 16, 256
+                    )
+            return carry
+
+        lax.fori_loop(0, 4, activate, 0)
+
+    activate_half(0, lanes)
+    activate_half(1, olanes)
 
     acc[...] = jnp.zeros_like(acc)
 
@@ -643,7 +655,7 @@
 
     for k in range(1, n_dec):
         lat_copy(k, d).wait_send()
-    for c in par_copies + stat_copies + [full, cw_copy, cw_pass, pm_full(0), pm_full(1)]:
+    for c in par_copies + stat_copies(0) + stat_copies(1) + [full, cw_copy, cw_pass, pm_full(0), pm_full(1)]:
         c.wait_send()
     if line:
 
@@ -782,8 +794,8 @@
             pltpu.VMEM((4, 3, 256, 512), BF16),
             pltpu.VMEM((2, 6, 6, 16, 128), BF16),
             pltpu.VMEM((4, 4, 5, 16, 512), BF16),
-            pltpu.VMEM((8, 512), F32),
-            pltpu.VMEM((n_row - 1, 8, 512), F32),
+            pltpu.VMEM((2, 8, 256), F32),
+            pltpu.VMEM((2, n_row - 1, 8, 256), F32),
             pltpu.VMEM((slots, 8, 16, 256), BF16),
             pltpu.VMEM((slots, 8, 16, 256), BF16),
             pltpu.VMEM((2, 8, 32, 256), BF16),
@@ -803,8 +815,8 @@
             dma((5,)),
             dma((2,)),
             dma((2,)),
-            dma((n_row - 1,)),
-            dma((n_row - 1,)),
+            dma((2, n_row - 1)),
+            dma((2, n_row - 1)),
             dma((2, 5)),
             dma((2, 5)),
         ],

time: 39.2 us -> 39.3 us (level)
  no operation moved by 1% of the time
where the time goes in v4:
time: 39.3 us; the launch traced here: 39.1 us
  Pallas kernels  38.5 us (98%)
  between operations  0.64 us (2%)
    pallas_call x1, Pallas kernels, shards(): pl.pallas_call(functools.partial(kernel, n_dec, n_row), out_shape=(jax.Sh...  36.1 us
    pallas_call x1, Pallas kernels, shards(): pl.pallas_call(weave_kernel, out_shape=(jax.ShapeDtypeStruct((2, 4, 8, 16...  2.37 us

profile of v4, /device:TPU:0, one launch (start us, length us, event | category | flops | bytes accessed | tf_op | source)
XLA Modules:
  0.0 39.1 jit_solution(9797848871960770819)
XLA Ops:
  0.6 36.1 %shard_map.148 = (bf16[4,2,4,32,256]{4,3,2,1,0:T(8,128)(2,1)}, bf16[2,4,16,128]{3,2,1,0:T(8,128)(2,1)}, bf16[2,2,4,32,256]{4,3,2,1,0:T(8,128)(2,1)}) custom-call(bf16[256,2560]{1,0:T(8,128)(2,1)} %bitcast.10, bf16[64,2560]{1,0:T(8,128)(2,1)} %bitcast.11, f32[1,64]{1,0:T(1,128)} %bitcast.17, bf16[2,2,8,16,16]{4,3,2,1,0:T(8,128)(2,1)} %lat.1, ...), custom_call_target="tpu_custom_call" | custom-call | flops 8999999488 | bytes 12000000 | tf_op jit(solution)/shard_map/pallas_call | solution.py:770
  36.8 2.4 %shard_map.149 = (bf16[2,4,8,16,256]{4,3,2,1,0:T(8,128)(2,1)}, bf16[2,2,8,16,16]{4,3,2,1,0:T(8,128)(2,1)}, bf16[2,2,8,16,256]{4,3,2,1,0:T(8,128)(2,1)}) custom-call(bf16[4,2,4,32,256]{4,3,2,1,0:T(8,128)(2,1)} %get-tuple-element.6.decoded_in, bf16[2,4,16,128]{3,2,1,0:T(8,128)(2,1)} %get-tuple-element.7.new_lat_in, ...), custom_call_target="tpu_custom_call" | custom-call | flops 30000000 | bytes 1600000 | tf_op jit(solution)/shard_map/pallas_call | solution.py:844

commit v5 on v4

--- a/solution.py
+++ b/solution.py
@@ -62,6 +62,8 @@
     stats_in,
     gm0,
     gm1,
+    gm2,
+    gm3,
     sel,
     pm,
     mb,
@@ -107,10 +109,14 @@
 
     load_hidden = pltpu.make_async_copy(hidden, hid_v, local_sem.at[0])
     load_hidden.start()
-    gm = (gm0, gm1)
+    gm = (gm0, gm1, gm2, gm3)
+
+    def chunk(c):
+        return mid.at[:, 1 - c // 2, 4 * (c % 2) : 4 * (c % 2) + 4]
+
     own_mid = [
-        pltpu.make_async_copy(mid.at[:, f], gm[f].at[pl.ds(2 * d, 2)], local_sem.at[1 + f])
-        for f in range(2)
+        pltpu.make_async_copy(chunk(c), gm[c].at[pl.ds(2 * d, 2)], local_sem.at[8 + c])
+        for c in range(4)
     ]
     for c in own_mid:
         c.start()
@@ -131,7 +137,7 @@
 
     def mid_copy(k, origin, f):
         return remote(
-            mid.at[:, f], gm[f].at[pl.ds(2 * origin, 2)], mid_s.at[k - 1, f], mid_r.at[k - 1, f],
+            chunk(f), gm[f].at[pl.ds(2 * origin, 2)], mid_s.at[k - 1, f], mid_r.at[k - 1, f],
             (s, lax.rem(d + k, n_dec), r),
         )
 
@@ -142,12 +148,12 @@
 
     def end_copy(f):
         return remote(
-            mid.at[:, f], gm[f].at[pl.ds(2 * d, 2)], hop_s.at[0, f], hop_r.at[0, f], (s, near, r)
+            chunk(f), gm[f].at[pl.ds(2 * d, 2)], hop_s.at[0, f], hop_r.at[0, f], (s, near, r)
         )
 
     def cross_copy(f):
         return remote(
-            mid.at[:, f], gm[f].at[pl.ds(2 * d, 2)], hop_s.at[1, f], hop_r.at[1, f], (s, 3 - d, r)
+            chunk(f), gm[f].at[pl.ds(2 * d, 2)], hop_s.at[1, f], hop_r.at[1, f], (s, 3 - d, r)
         )
 
     def pass_copy(f):
@@ -212,21 +218,27 @@
     for k in range(1, n_dec):
         lat_copy(k, d).start()
 
-    if line:
-
-        @pl.when(inner)
-        def _():
-            for f in (1, 0):
-                cross_copy(f).start()
-
-        @pl.when(jnp.logical_not(inner))
-        def _():
-            for f in (1, 0):
-                end_copy(f).start()
-
-    else:
+    def send_end(*chunks):
+        if line:
+
+            @pl.when(jnp.logical_not(inner))
+            def _():
+                for c in chunks:
+                    end_copy(c).start()
+
+    def send_cross(*chunks):
+        if line:
+
+            @pl.when(inner)
+            def _():
+                for c in chunks:
+                    cross_copy(c).start()
+
+    send_end(0)
+    send_cross(0, 1)
+    if not line:
         for k in range(1, n_dec):
-            for f in (1, 0):
+            for f in range(4):
                 mid_copy(k, d, f).start()
 
     load_hidden.wait()
@@ -269,6 +281,7 @@
             c.start()
 
     full.start()
+    send_end(1)
 
     zero_slab = jnp.zeros((CZ, 256), BF16)
 
@@ -311,9 +324,12 @@
     def _():
         lat_edge_down.start()
 
+    send_end(2)
+    send_cross(2)
     cw_copy.wait_recv()
     cw_pass.start()
-    pass_on(1)
+    pass_on(0)
+    send_end(3)
 
     full.wait_recv()
 
@@ -375,6 +391,8 @@
 
     out_lat = pltpu.make_async_copy(nl_v, new_lat, local_sem.at[4])
     out_lat.start()
+    pass_on(1)
+    send_cross(3)
 
     def input_conv(pp, qq, row, count, part_lanes):
         out = jnp.zeros((64 * count, 256), F32)
@@ -425,7 +443,7 @@
                 input_conv(pp, qq, 0 if pp == 1 else 4, 1, part_lanes)
 
     input_half(0, lanes)
-    pass_on(0)
+    pass_on(2)
     cw_pass.wait_recv()
     build(cw_in, olanes)
     for n, ref in enumerate((cb, gain, gbias)):
@@ -442,37 +460,44 @@
     def _():
         pm[:, 9] = zero_row
 
-    def pm_full(f):
-        block = pm.at[f, 1:9, :, lanes]
-        return remote(block, block, pm_s.at[f, 0], pm_r.at[f, 0], (o, d, r))
-
-    def pm_up(f):
+    def pm_full(c):
+        low = 1 + 4 * (c % 2)
+        block = pm.at[1 - c // 2, low : low + 4, :, lanes]
+        return remote(block, block, pm_s.at[c, 0], pm_r.at[c, 0], (o, d, r))
+
+    def pm_up(c):
+        f = 1 - c // 2
         return [
-            remote(pm.at[f, 1, :, lanes], pm.at[f, 9, :, lanes], pm_s.at[f, 1 + n], pm_r.at[f, 1 + n], (dev, d, r - 1))
+            remote(pm.at[f, 1, :, lanes], pm.at[f, 9, :, lanes], pm_s.at[c, 1 + n], pm_r.at[c, 1 + n], (dev, d, r - 1))
             for n, dev in enumerate((s, o))
         ]
 
-    def pm_down(f):
+    def pm_down(c):
+        f = 1 - c // 2
         return [
-            remote(pm.at[f, 8, :, lanes], pm.at[f, 0, :, lanes], pm_s.at[f, 3 + n], pm_r.at[f, 3 + n], (dev, d, r + 1))
+            remote(pm.at[f, 8, :, lanes], pm.at[f, 0, :, lanes], pm_s.at[c, 1 + n], pm_r.at[c, 1 + n], (dev, d, r + 1))
             for n, dev in enumerate((s, o))
         ]
 
-    def share(f, pick):
+    def share(c, pick):
+        low = 1 + 4 * (c % 2)
         for st in range(2):
             live = (span[st] > 0).astype(BF16)
-            pm[f, 1:9, pl.ds(16 * st, 16), lanes] = pick(st) * live
-        pm_full(f).start()
-
-        @pl.when(has_up)
-        def _():
-            for c in pm_up(f):
-                c.start()
-
-        @pl.when(has_down)
-        def _():
-            for c in pm_down(f):
-                c.start()
+            pm[1 - c // 2, low : low + 4, pl.ds(16 * st, 16), lanes] = pick(st) * live
+        pm_full(c).start()
+        if c % 2 == 0:
+
+            @pl.when(has_up)
+            def _():
+                for e in pm_up(c):
+                    e.start()
+
+        else:
+
+            @pl.when(has_down)
+            def _():
+                for e in pm_down(c):
+                    e.start()
 
     def share_inner(f):
         if line:
@@ -501,7 +526,8 @@
                 mid_copy(k, lax.rem(d + n_dec - k, n_dec), f).wait_recv()
             share(f, lambda st: gm[f][moves[2 * d + st]])
 
-    share_inner(1)
+    pass_on(3)
+    share_inner(0)
 
     def activate_half(n, part_lanes):
         for c in stat_copies(n):
@@ -547,7 +573,10 @@
         lax.fori_loop(0, 4, activate, 0)
 
     activate_half(0, lanes)
+    share_inner(1)
     activate_half(1, olanes)
+    share_inner(2)
+    share_end(0)
 
     acc[...] = jnp.zeros_like(acc)
 
@@ -572,7 +601,6 @@
             got = jnp.dot(lhs, midw_v[a * 3 + b], preferred_element_type=F32)
             acc[:, t0 : t0 + nt] += got.reshape(4, nt, 64, 256)
 
-    share_inner(0)
     load_w.wait()
 
     def tap_late(b, carry):
@@ -580,10 +608,12 @@
         return carry
 
     lax.fori_loop(0, 1, tap_late, 0)
+    share_inner(3)
     share_end(1)
     lax.fori_loop(1, 2, tap_late, 0)
-    share_end(0)
+    share_end(2)
     lax.fori_loop(2, 3, tap_late, 0)
+    share_end(3)
 
     def tap_mid(k, carry):
         conv(k, ((1, 1, 3), (0, 2, 2)))
@@ -624,16 +654,18 @@
     out_late.start()
 
     for f, pairs in ((1, ((1, 0, 1), (0, 1, 1))), (0, ((0, 0, 1),))):
-        pm_full(f).wait_recv()
+        first = 2 - 2 * f
+        pm_full(first).wait_recv()
+        pm_full(first + 1).wait_recv()
 
         @pl.when(has_up)
         def _():
-            for c in pm_down(f):
+            for c in pm_down(first + 1):
                 c.wait_recv()
 
         @pl.when(has_down)
         def _():
-            for c in pm_up(f):
+            for c in pm_up(first):
                 c.wait_recv()
 
         for row in range(10):
@@ -655,36 +687,36 @@
 
     for k in range(1, n_dec):
         lat_copy(k, d).wait_send()
-    for c in par_copies + stat_copies(0) + stat_copies(1) + [full, cw_copy, cw_pass, pm_full(0), pm_full(1)]:
+    for c in par_copies + stat_copies(0) + stat_copies(1) + [full, cw_copy, cw_pass] + [pm_full(c) for c in range(4)]:
         c.wait_send()
     if line:
 
         @pl.when(inner)
         def _():
-            for f in range(2):
+            for f in range(4):
                 cross_copy(f).wait_send()
                 pass_copy(f).wait_send()
                 pick_copy(f, end).wait_send()
 
         @pl.when(jnp.logical_not(inner))
         def _():
-            for f in range(2):
+            for f in range(4):
                 end_copy(f).wait_send()
                 own_mid[f].wait()
 
     else:
         for k in range(1, n_dec):
-            for f in range(2):
+            for f in range(4):
                 mid_copy(k, d, f).wait_send()
 
     @pl.when(has_up)
     def _():
-        for c in up + pm_up(0) + pm_up(1) + [lat_edge_up]:
+        for c in up + pm_up(0) + pm_up(2) + [lat_edge_up]:
             c.wait_send()
 
     @pl.when(has_down)
     def _():
-        for c in down + pm_down(0) + pm_down(1) + [lat_edge_down]:
+        for c in down + pm_down(1) + pm_down(3) + [lat_edge_down]:
             c.wait_send()
     for c in (out_lat, out_mid, out_late, out_early):
         c.wait()
@@ -796,19 +828,21 @@
             pltpu.VMEM((4, 4, 5, 16, 512), BF16),
             pltpu.VMEM((2, 8, 256), F32),
             pltpu.VMEM((2, n_row - 1, 8, 256), F32),
-            pltpu.VMEM((slots, 8, 16, 256), BF16),
-            pltpu.VMEM((slots, 8, 16, 256), BF16),
-            pltpu.VMEM((2, 8, 32, 256), BF16),
+            pltpu.VMEM((slots, 4, 16, 256), BF16),
+            pltpu.VMEM((slots, 4, 16, 256), BF16),
+            pltpu.VMEM((slots, 4, 16, 256), BF16),
+            pltpu.VMEM((slots, 4, 16, 256), BF16),
+            pltpu.VMEM((4, 4, 32, 256), BF16),
             pltpu.VMEM((2, 10, 32, 512), BF16),
             pltpu.VMEM((2, 4, 6, 5, 16, 512), BF16),
             pltpu.VMEM((4, 4, 64, 256), F32),
-            dma((8,)),
+            dma((12,)),
             dma((n_dec - 1,)),
             dma((n_dec - 1,)),
-            dma((n_dec - 1, 2)),
-            dma((n_dec - 1, 2)),
-            dma((4, 2)),
-            dma((4, 2)),
+            dma((n_dec - 1, 4)),
+            dma((n_dec - 1, 4)),
+            dma((4, 4)),
+            dma((4, 4)),
             dma((5,)),
             dma((5,)),
             dma((5,)),
@@ -817,8 +851,8 @@
             dma((2,)),
             dma((2, n_row - 1)),
             dma((2, n_row - 1)),
-            dma((2, 5)),
-            dma((2, 5)),
+            dma((4, 3)),
+            dma((4, 3)),
         ],
         compiler_params=pltpu.CompilerParams(
             collective_id=0, has_side_effects=True, vmem_limit_bytes=56 * 1024 * 1024

time: 39.3 us -> 37.7 us (0.959)
  Pallas kernels: 38.5 us -> 36.9 us
    pallas_call x1, Pallas kernels: 36.1 us -> 34.5 us  [shards(): pl.pallas_call(functools.partial(kernel, n_dec, n_row), out_shape=(jax.Sh...]
where the time goes in v5:
time: 37.7 us; the launch traced here: 37.5 us
  Pallas kernels  36.9 us (98%)
  between operations  0.64 us (2%)
    pallas_call x1, Pallas kernels, shards(): pl.pallas_call(functools.partial(kernel, n_dec, n_row), out_shape=(jax.Sh...  34.5 us
    pallas_call x1, Pallas kernels, shards(): pl.pallas_call(weave_kernel, out_shape=(jax.ShapeDtypeStruct((2, 4, 8, 16...  2.37 us

profile of v5, /device:TPU:0, one launch (start us, length us, event | category | flops | bytes accessed | tf_op | source)
XLA Modules:
  0.0 37.5 jit_solution(8105962781798623698)
XLA Ops:
  0.6 34.5 %shard_map.148 = (bf16[4,2,4,32,256]{4,3,2,1,0:T(8,128)(2,1)}, bf16[2,4,16,128]{3,2,1,0:T(8,128)(2,1)}, bf16[2,2,4,32,256]{4,3,2,1,0:T(8,128)(2,1)}) custom-call(bf16[256,2560]{1,0:T(8,128)(2,1)} %bitcast.10, bf16[64,2560]{1,0:T(8,128)(2,1)} %bitcast.11, f32[1,64]{1,0:T(1,128)} %bitcast.17, bf16[2,2,8,16,16]{4,3,2,1,0:T(8,128)(2,1)} %lat.1, ...), custom_call_target="tpu_custom_call" | custom-call | flops 8999999488 | bytes 12000000 | tf_op jit(solution)/shard_map/pallas_call | solution.py:802
  35.2 2.4 %shard_map.149 = (bf16[2,4,8,16,256]{4,3,2,1,0:T(8,128)(2,1)}, bf16[2,2,8,16,16]{4,3,2,1,0:T(8,128)(2,1)}, bf16[2,2,8,16,256]{4,3,2,1,0:T(8,128)(2,1)}) custom-call(bf16[4,2,4,32,256]{4,3,2,1,0:T(8,128)(2,1)} %get-tuple-element.6.decoded_in, bf16[2,4,16,128]{3,2,1,0:T(8,128)(2,1)} %get-tuple-element.7.new_lat_in, ...), custom_call_target="tpu_custom_call" | custom-call | flops 30000000 | bytes 1600000 | tf_op jit(solution)/shard_map/pallas_call | solution.py:878

commit v6 on v5

--- a/solution.py
+++ b/solution.py
@@ -541,8 +541,8 @@
             sums = sums + other
         sums = sums / (4 * 8 * 16 * GROUP * n_row)
         gv = sums[2:4] - sums[0:2] * sums[0:2]
-        scale = lax.rsqrt(gv + 1e-5) * par_all[1, :, part_lanes]
-        shift = par_all[2, :, part_lanes]
+        scale = 0.5 * (lax.rsqrt(gv + 1e-5) * par_all[1, :, part_lanes])
+        shift = 0.5 * par_all[2, :, part_lanes]
 
         def spread(v):
             return jnp.concatenate(
@@ -555,16 +555,10 @@
         def activate(t, carry):
             for pp in range(2):
                 for qq in range(2):
-                    v = (h1[pp * 2 + qq, t, :, :, part_lanes].astype(F32) - mean16) * scale16 + shift
-                    v = v * (0.5 * jnp.tanh(0.5 * v) + 0.5)
-                    edge = lax.broadcasted_iota(jnp.int32, (5, 16, 256), 0)
-                    if pp == 1:
-                        v = jnp.where((edge == 0) & jnp.logical_not(has_up), 0.0, v)
-                    else:
-                        v = jnp.where((edge == 4) & jnp.logical_not(has_down), 0.0, v)
-                    v = v.astype(BF16)
-                    mb[pp, qq, t + 2, :, :, part_lanes] = v
-                    moved = shifted(v.astype(F32).reshape(80, 256), -1 if qq == 1 else 1)
+                    u = (h1[pp * 2 + qq, t, :, :, part_lanes].astype(F32) - mean16) * scale16 + shift
+                    v = u * jnp.tanh(u) + u
+                    mb[pp, qq, t + 2, :, :, part_lanes] = v.astype(BF16)
+                    moved = shifted(v.reshape(80, 256), -1 if qq == 1 else 1)
                     mb[pp, 2 if qq == 1 else 3, t + 2, :, :, part_lanes] = moved.astype(BF16).reshape(
                         5, 16, 256
                     )
@@ -575,6 +569,15 @@
     activate_half(0, lanes)
     share_inner(1)
     activate_half(1, olanes)
+
+    @pl.when(jnp.logical_not(has_up))
+    def _():
+        mb[1, :, 2:6, 0] = jnp.zeros((4, 4, 16, 512), BF16)
+
+    @pl.when(jnp.logical_not(has_down))
+    def _():
+        mb[0, :, 2:6, 4] = jnp.zeros((4, 4, 16, 512), BF16)
+
     share_inner(2)
     share_end(0)
 
@@ -582,11 +585,13 @@
 
     def conv(b, pairs):
         for a, t0, nt in pairs:
-            pieces = []
-            for pp in range(2):
-                src = (b + 1) % 2 if pp == 0 else b % 2
-                off = b // 2 if pp == 0 else (b + 1) // 2
-                for qq in range(2):
+            joined = 1 if nt == 4 else 4 if nt == 1 else 2
+            for low in range(0, 4, joined):
+                pieces = []
+                for n in range(low, low + joined):
+                    pp, qq = n // 2, n % 2
+                    src = (b + 1) % 2 if pp == 0 else b % 2
+                    off = b // 2 if pp == 0 else (b + 1) // 2
                     taps = (2, 0, 1) if qq == 0 else (0, 1, 3)
                     pieces.append(
                         jnp.concatenate(
@@ -597,9 +602,9 @@
                             axis=1,
                         )
                     )
-            lhs = jnp.concatenate(pieces, axis=0)
-            got = jnp.dot(lhs, midw_v[a * 3 + b], preferred_element_type=F32)
-            acc[:, t0 : t0 + nt] += got.reshape(4, nt, 64, 256)
+                lhs = pieces[0] if joined == 1 else jnp.concatenate(pieces, axis=0)
+                got = jnp.dot(lhs, midw_v[a * 3 + b], preferred_element_type=F32)
+                acc[low : low + joined, t0 : t0 + nt] += got.reshape(joined, nt, 64, 256)
 
     load_w.wait()
 

time: 37.7 us -> 37.4 us (level)
  no operation moved by 1% of the time
where the time goes in v6:
time: 37.4 us; the launch traced here: 37.3 us
  Pallas kernels  36.6 us (98%)
  between operations  0.64 us (2%)
    pallas_call x1, Pallas kernels, shards(): pl.pallas_call(functools.partial(kernel, n_dec, n_row), out_shape=(jax.Sh...  34.3 us
    pallas_call x1, Pallas kernels, shards(): pl.pallas_call(weave_kernel, out_shape=(jax.ShapeDtypeStruct((2, 4, 8, 16...  2.37 us

profile of v6, /device:TPU:0, one launch (start us, length us, event | category | flops | bytes accessed | tf_op | source)
XLA Modules:
  0.0 37.3 jit_solution(816741449383424925)
XLA Ops:
  0.6 34.3 %shard_map.148 = (bf16[4,2,4,32,256]{4,3,2,1,0:T(8,128)(2,1)}, bf16[2,4,16,128]{3,2,1,0:T(8,128)(2,1)}, bf16[2,2,4,32,256]{4,3,2,1,0:T(8,128)(2,1)}) custom-call(bf16[256,2560]{1,0:T(8,128)(2,1)} %bitcast.10, bf16[64,2560]{1,0:T(8,128)(2,1)} %bitcast.11, f32[1,64]{1,0:T(1,128)} %bitcast.17, bf16[2,2,8,16,16]{4,3,2,1,0:T(8,128)(2,1)} %lat.1, ...), custom_call_target="tpu_custom_call" | custom-call | flops 8999999488 | bytes 12000000 | tf_op jit(solution)/shard_map/pallas_call | solution.py:807
  34.9 2.4 %shard_map.149 = (bf16[2,4,8,16,256]{4,3,2,1,0:T(8,128)(2,1)}, bf16[2,2,8,16,16]{4,3,2,1,0:T(8,128)(2,1)}, bf16[2,2,8,16,256]{4,3,2,1,0:T(8,128)(2,1)}) custom-call(bf16[4,2,4,32,256]{4,3,2,1,0:T(8,128)(2,1)} %get-tuple-element.6.decoded_in, bf16[2,4,16,128]{3,2,1,0:T(8,128)(2,1)} %get-tuple-element.7.new_lat_in, ...), custom_call_target="tpu_custom_call" | custom-call | flops 30000000 | bytes 1600000 | tf_op jit(solution)/shard_map/pallas_call | solution.py:883

commit v7 on v6

--- a/solution.py
+++ b/solution.py
@@ -728,12 +728,25 @@
 
 
 def weave_kernel(
-    decoded_in, new_lat_in, new_mid_in, decoded_out, new_lat_out, new_mid_out, decoded, new_lat, new_mid, sem
+    decoded_in,
+    new_lat_in,
+    new_mid_in,
+    decoded_hbm,
+    new_lat_out,
+    new_mid_hbm,
+    decoded,
+    new_lat,
+    new_mid,
+    decoded_out,
+    new_mid_out,
+    sem,
 ):
     loads = [
         pltpu.make_async_copy(source, target, sem.at[n])
         for n, (source, target) in enumerate(
-            ((new_lat_in, new_lat), (new_mid_in, new_mid), (decoded_in, decoded))
+            [(new_mid_in, new_mid)]
+            + [(decoded_in.at[t], decoded.at[t]) for t in range(4)]
+            + [(new_lat_in, new_lat)]
         )
     ]
     for c in loads:
@@ -750,6 +763,19 @@
                 target[1, t, 2 * i + pp] = y[16:32]
 
     loads[0].wait()
+    for t in range(2):
+        spread(new_mid, new_mid_out, t)
+    stores = [pltpu.make_async_copy(new_mid_out, new_mid_hbm, sem.at[6])]
+    stores[0].start()
+    for t in range(4):
+        loads[1 + t].wait()
+        spread(decoded, decoded_out, t)
+        stores.append(
+            pltpu.make_async_copy(decoded_out.at[:, t], decoded_hbm.at[:, t], sem.at[7 + t])
+        )
+        stores[-1].start()
+    loads[5].wait()
+
     patches = new_lat[...].reshape(128, 128)
     ro = lax.broadcasted_iota(jnp.int32, (256, 128), 0)
     co = lax.broadcasted_iota(jnp.int32, (256, 128), 1)
@@ -773,12 +799,8 @@
                 for st in range(2):
                     row = ((t * 4 + i) * 2 + st) * 16
                     new_lat_out[st, t, 2 * i + p] = y[row : row + 16]
-    loads[1].wait()
-    for t in range(2):
-        spread(new_mid, new_mid_out, t)
-    loads[2].wait()
-    for t in range(4):
-        spread(decoded, decoded_out, t)
+    for c in stores:
+        c.wait()
 
 
 def shards(
@@ -888,12 +910,14 @@
             jax.ShapeDtypeStruct((2, 2, 8, 16, 256), BF16),
         ),
         in_specs=[hbm, hbm, hbm],
-        out_specs=(vm, vm, vm),
+        out_specs=(hbm, vm, hbm),
         scratch_shapes=[
             pltpu.VMEM((4, 2, 4, 32, 256), BF16),
             pltpu.VMEM((2, 4, 16, 128), BF16),
             pltpu.VMEM((2, 2, 4, 32, 256), BF16),
-            dma((3,)),
+            pltpu.VMEM((2, 4, 8, 16, 256), BF16),
+            pltpu.VMEM((2, 2, 8, 16, 256), BF16),
+            dma((11,)),
         ],
         compiler_params=pltpu.CompilerParams(vmem_limit_bytes=60 * 1024 * 1024),
         cost_estimate=pl.CostEstimate(flops=30_000_000, bytes_accessed=1_600_000, transcendentals=0),

time: 37.4 us -> 38.3 us (1.024)
  Pallas kernels: 36.6 us -> 37.5 us
    pallas_call x1, Pallas kernels: 2.37 us -> 3.22 us  [shards(): pl.pallas_call(weave_kernel, out_shape=(jax.ShapeDtypeStruct((2, 4, 8, 16...]
where the time goes in v7:
time: 38.3 us; the launch traced here: 38.1 us
  Pallas kernels  37.5 us (98%)
  between operations  0.64 us (2%)
    pallas_call x1, Pallas kernels, shards(): pl.pallas_call(functools.partial(kernel, n_dec, n_row), out_shape=(jax.Sh...  34.3 us
    pallas_call x1, Pallas kernels, shards(): pl.pallas_call(weave_kernel, out_shape=(jax.ShapeDtypeStruct((2, 4, 8, 16...  3.22 us

profile of v7, /device:TPU:0, one launch (start us, length us, event | category | flops | bytes accessed | tf_op | source)
XLA Modules:
  0.0 38.1 jit_solution(10355213359208801674)
XLA Ops:
  0.6 34.3 %shard_map.148 = (bf16[4,2,4,32,256]{4,3,2,1,0:T(8,128)(2,1)}, bf16[2,4,16,128]{3,2,1,0:T(8,128)(2,1)}, bf16[2,2,4,32,256]{4,3,2,1,0:T(8,128)(2,1)}) custom-call(bf16[256,2560]{1,0:T(8,128)(2,1)} %bitcast.10, bf16[64,2560]{1,0:T(8,128)(2,1)} %bitcast.11, f32[1,64]{1,0:T(1,128)} %bitcast.17, bf16[2,2,8,16,16]{4,3,2,1,0:T(8,128)(2,1)} %lat.1, ...), custom_call_target="tpu_custom_call" | custom-call | flops 8999999488 | bytes 12000000 | tf_op jit(solution)/shard_map/pallas_call | solution.py:829
  34.9 3.2 %shard_map.149 = (bf16[2,4,8,16,256]{4,3,2,1,0:T(8,128)(2,1)}, bf16[2,2,8,16,16]{4,3,2,1,0:T(8,128)(2,1)}, bf16[2,2,8,16,256]{4,3,2,1,0:T(8,128)(2,1)}) custom-call(bf16[4,2,4,32,256]{4,3,2,1,0:T(8,128)(2,1)} %get-tuple-element.6.decoded_in, bf16[2,4,16,128]{3,2,1,0:T(8,128)(2,1)} %get-tuple-element.7.new_lat_in, ...), custom_call_target="tpu_custom_call" | custom-call | flops 30000000 | bytes 1600000 | tf_op jit(solution)/shard_map/pallas_call | solution.py:905
